TPU v7x, 256 devices: a whole 4x4x8 slice. The times are simulated.
256 devices in a mesh: lon: 16 (over z, core), lat: 8 (over y, x_lo), tp: 2 (over x_hi).
Axes of the slice: x: 4 (x_hi: 2, x_lo: 2; x = x_hi * 2 + x_lo), y: 4, z: 8, core: 2. Of those that a mesh axis runs over, the one named last changes fastest.
Arguments:
- latent: bfloat16 [2, 48, 768, 512], P(None, 'lat', 'lon'), may hold values from -6 to 6
- pole_mask: int32 [48], replicated, may hold values from 0 to 1, as said below
- attn_gain: float32 [512], replicated, may hold values from 0.25 to 1.75
- qkv_weight: bfloat16 [512, 3, 512], P(None, None, 'tp'), may hold values from -0.44194174 to 0.44194174
- proj_weight: bfloat16 [512, 512], P('tp'), may hold values from -0.25 to 0.25
- rel_bias: float32 [8, 759], P('tp'), may hold values from -4 to 4
- merge_gain: float32 [2048], replicated, may hold values from 0.25 to 1.75
- merge_weight: bfloat16 [2048, 1024], P(None, 'tp'), may hold values from -0.125 to 0.125
- coarse_grad: bfloat16 [2, 24, 384, 1024], P(None, 'lat', 'lon', 'tp'), may hold values from -6 to 6
Outputs:
- latent_grad: bfloat16 [2, 48, 768, 512], P(None, 'lat', 'lon')
- attn_gain_grad: float32 [512], replicated
- qkv_weight_grad: float32 [512, 3, 512], P(('lon', 'lat'), None, 'tp')
- proj_weight_grad: float32 [512, 512], P('tp', ('lon', 'lat'))
- rel_bias_grad: float32 [8, 759], P('tp')
- merge_gain_grad: float32 [2048], replicated
- merge_weight_grad: float32 [2048, 1024], P(('lon', 'lat'), 'tp')
Inputs may be any that keep to these rules, and one draw needn't show every extreme that they name: `pole_mask`: between 1 and 2 rows at each end of the 48 rows are 0, all others 1.
All inputs are finite; a program needn't handle non-finite values.
Results may differ from a plain program's by a relative error of at most 0.025.
Values may be sent and summed in bfloat16 or wider, within the bound.
A program may use at most 128 MiB of HBM per device.

v0:
```python
import jax
import jax.numpy as jnp
from jax import lax
from jax.sharding import PartitionSpec as P

WLAT = 6
WLON = 12


EPS = 1e-05
NEG = -1e30


def shifted_2(block, axis, distance):
    devices = range(lax.axis_size(axis))
    route = [((i - distance) % len(devices), i) for i in devices]
    return lax.ppermute(block, axis, route)


def layer_stats(inputs):
    center = inputs - jnp.mean(inputs, -1, keepdims=True)
    spread = jnp.mean(center * center, -1, keepdims=True)
    inverse = lax.rsqrt(spread + EPS)
    return (center * inverse, inverse)


def norm_back(upstream, gain, normed, inverse):
    scaled = upstream * gain
    return inverse * (
        scaled
        - jnp.mean(scaled, -1, keepdims=True)
        - normed * jnp.mean(scaled * normed, -1, keepdims=True)
    )


def to_windows(grid, win_lat, win_lon):
    levels, lat_rows, lon_cols, features = grid.shape
    grid = grid.reshape(
        levels, lat_rows // win_lat, win_lat, lon_cols // win_lon, win_lon, features
    )
    return grid.transpose(1, 3, 0, 2, 4, 5).reshape(-1, levels * win_lat * win_lon, features)


def from_windows(blocks, levels, lat_rows, lon_cols, win_lat, win_lon):
    features = blocks.shape[-1]
    blocks = blocks.reshape(
        lat_rows // win_lat, lon_cols // win_lon, levels, win_lat, win_lon, features
    )
    return blocks.transpose(2, 0, 3, 1, 4, 5).reshape(levels, lat_rows, lon_cols, features)


def merge_patches(grid):
    levels, lat_rows, lon_cols, features = grid.shape
    grid = grid.reshape(levels, lat_rows // 2, 2, lon_cols // 2, 2, features).transpose(
        0, 1, 3, 2, 4, 5
    )
    return grid.reshape(levels, lat_rows // 2, lon_cols // 2, 4 * features)


def split_patches(grid):
    levels, half_rows, half_cols, features = grid.shape
    grid = grid.reshape(levels, half_rows, half_cols, 2, 2, features // 4).transpose(
        0, 1, 3, 2, 4, 5
    )
    return grid.reshape(levels, 2 * half_rows, 2 * half_cols, features // 4)


def relative_index(levels, win_lat, win_lon):
    position = jnp.arange(levels * win_lat * win_lon, dtype=jnp.int32)
    level_of = position // (win_lat * win_lon)
    row_of = position // win_lon % win_lat
    col_of = position % win_lon
    level_gap = level_of[:, None] - level_of[None, :] + levels - 1
    row_gap = row_of[:, None] - row_of[None, :] + win_lat - 1
    col_gap = col_of[:, None] - col_of[None, :] + win_lon - 1
    return (level_gap * (2 * win_lat - 1) + row_gap) * (2 * win_lon - 1) + col_gap


def roll_in(grid, half_lat, half_lon):
    arrived = shifted_2(grid[:, :, -half_lon:], "lon", 1)
    grid = jnp.concatenate([arrived, grid[:, :, :-half_lon]], 2)
    arrived = shifted_2(grid[:, -half_lat:], "lat", 1)
    return jnp.concatenate([arrived, grid[:, :-half_lat]], 1)


def roll_out(grid, half_lat, half_lon):
    arrived = shifted_2(grid[:, :, :half_lon], "lon", -1)
    grid = jnp.concatenate([grid[:, :, half_lon:], arrived], 2)
    arrived = shifted_2(grid[:, :half_lat], "lat", -1)
    return jnp.concatenate([grid[:, half_lat:], arrived], 1)


def local(
    latent,
    pole_mask,
    attn_gain,
    qkv_weight,
    proj_weight,
    rel_bias,
    merge_gain,
    merge_weight,
    coarse_grad,
):
    levels, lat_rows, lon_cols, features = latent.shape
    heads_here = rel_bias.shape[0]
    local_cols = qkv_weight.shape[2]
    head_size = local_cols // heads_here
    scale = head_size ** (-0.5)
    half_lat = WLAT // 2
    half_lon = WLON // 2
    data_devices = lax.axis_size("lon") * lax.axis_size("lat")
    total_rows = lat_rows * lax.axis_size("lat")
    token_count = levels * lat_rows * lon_cols
    rel = relative_index(levels, WLAT, WLON)
    bias_block = jnp.take(rel_bias, rel, axis=1)
    shifted_rows = lax.axis_index("lat") * lat_rows + jnp.arange(lat_rows, dtype=jnp.int32)
    source_rows = (shifted_rows - half_lat) % total_rows
    matches = source_rows[:, None] == jnp.arange(total_rows, dtype=jnp.int32)[None, :]
    rows_valid = jnp.sum(jnp.where(matches, pole_mask[None, :], 0), 1) > 0
    rows_side = shifted_rows < half_lat
    grid_valid = jnp.broadcast_to(rows_valid[None, :, None, None], (levels, lat_rows, lon_cols, 1))
    grid_side = jnp.broadcast_to(rows_side[None, :, None, None], (levels, lat_rows, lon_cols, 1))
    valid_w = to_windows(grid_valid, WLAT, WLON)[..., 0]
    side_w = to_windows(grid_side, WLAT, WLON)[..., 0]
    allowed = valid_w[:, None, :] & (side_w[:, :, None] == side_w[:, None, :])
    shifted = roll_in(latent, half_lat, half_lon)
    x_float = shifted.reshape(token_count, features).astype(jnp.float32)
    normed, inverse = layer_stats(x_float)
    hidden = (normed * attn_gain).astype(jnp.bfloat16)
    w_flat = qkv_weight.reshape(features, 3 * local_cols)
    qkv = jnp.dot(hidden, w_flat, preferred_element_type=jnp.float32).astype(jnp.bfloat16)
    qkv_w = to_windows(qkv.reshape(levels, lat_rows, lon_cols, 3 * local_cols), WLAT, WLON)
    windows, wtok = (qkv_w.shape[0], qkv_w.shape[1])
    qkv_w = qkv_w.reshape(windows, wtok, 3, heads_here, head_size)
    query, keys, values = (qkv_w[:, :, 0], qkv_w[:, :, 1], qkv_w[:, :, 2])
    scores = (
        jnp.einsum("wqhd,wkhd->whqk", query, keys, preferred_element_type=jnp.float32) * scale
        + bias_block[None]
    )
    scores = jnp.where(allowed[:, None], scores, NEG)
    highest = jnp.max(scores, -1, keepdims=True)
    expd = jnp.exp(scores - highest)
    prob = expd / jnp.sum(expd, -1, keepdims=True)
    prob_b = prob.astype(jnp.bfloat16)
    out_w = jnp.einsum(
        "whqk,wkhd->wqhd", prob_b, values, preferred_element_type=jnp.float32
    ).astype(jnp.bfloat16)
    attn_o = from_windows(
        out_w.reshape(windows, wtok, local_cols), levels, lat_rows, lon_cols, WLAT, WLON
    ).reshape(token_count, local_cols)
    attn_out = lax.psum(
        jnp.dot(attn_o, proj_weight, preferred_element_type=jnp.float32).astype(jnp.bfloat16), "tp"
    ).astype(jnp.float32)
    out_flat = (x_float + attn_out).astype(jnp.bfloat16)
    out_shifted = out_flat.reshape(levels, lat_rows, lon_cols, features)
    out_grid = roll_out(out_shifted, half_lat, half_lon)
    merged = merge_patches(out_grid).astype(jnp.float32)
    merge_hat, merge_inv = layer_stats(merged)
    merge_hat = merge_hat.reshape(-1, 4 * features)
    merged_b = (merge_hat * merge_gain).astype(jnp.bfloat16)
    coarse_flat = coarse_grad.reshape(-1, coarse_grad.shape[-1])
    d_partial = lax.dot_general(
        coarse_flat, merge_weight, (((1,), (1,)), ((), ())), preferred_element_type=jnp.float32
    )
    d_merged = lax.psum(d_partial.astype(jnp.bfloat16), "tp").astype(jnp.float32)
    columns = merged_b
    merge_weight_grad = lax.psum_scatter(
        lax.dot_general(
            columns, coarse_flat, (((0,), (0,)), ((), ())), preferred_element_type=jnp.float32
        ),
        ("lon", "lat"),
        scatter_dimension=0,
        tiled=True,
    )
    merge_gain_part = jnp.sum(d_merged * merge_hat, 0)
    d_fine = norm_back(d_merged, merge_gain, merge_hat, merge_inv.reshape(-1, 1)).reshape(
        merged.shape
    )
    d_fine = split_patches(d_fine)
    grad_shift = roll_in(d_fine.astype(jnp.bfloat16), half_lat, half_lon).reshape(
        token_count, features
    )
    d_out = lax.dot_general(
        grad_shift, proj_weight, (((1,), (1,)), ((), ())), preferred_element_type=jnp.float32
    ).astype(jnp.bfloat16)
    proj_term = lax.dot_general(
        attn_o, grad_shift, (((0,), (0,)), ((), ())), preferred_element_type=jnp.float32
    )
    proj_weight_grad = lax.psum_scatter(proj_term, ("lon", "lat"), scatter_dimension=1, tiled=True)
    d_out_w = to_windows(d_out.reshape(levels, lat_rows, lon_cols, local_cols), WLAT, WLON).reshape(
        windows, wtok, heads_here, head_size
    )
    d_prob = jnp.einsum("wqhd,wkhd->whqk", d_out_w, values, preferred_element_type=jnp.float32)
    d_values = jnp.einsum("whqk,wqhd->wkhd", prob_b, d_out_w, preferred_element_type=jnp.float32)
    d_scores = prob * (d_prob - jnp.sum(d_prob * prob, -1, keepdims=True))
    score_total = jnp.sum(d_scores, 0).reshape(heads_here, -1)
    bias_part = jax.ops.segment_sum(score_total.T, rel.reshape(-1), rel_bias.shape[1]).T
    d_scores_b = d_scores.astype(jnp.bfloat16)
    d_query = (
        jnp.einsum("whqk,wkhd->wqhd", d_scores_b, keys, preferred_element_type=jnp.float32) * scale
    )
    d_keys = (
        jnp.einsum("whqk,wqhd->wkhd", d_scores_b, query, preferred_element_type=jnp.float32) * scale
    )
    d_qkv_w = (
        jnp.stack([d_query, d_keys, d_values], 2)
        .astype(jnp.bfloat16)
        .reshape(windows, wtok, 3 * local_cols)
    )
    d_qkv = from_windows(d_qkv_w, levels, lat_rows, lon_cols, WLAT, WLON).reshape(
        token_count, 3 * local_cols
    )
    columns = hidden
    product = lax.dot_general(
        columns, d_qkv, (((0,), (0,)), ((), ())), preferred_element_type=jnp.float32
    )
    qkv_weight_grad = lax.psum_scatter(
        product.reshape(features // data_devices * lax.axis_size(("lon", "lat")), 3, local_cols),
        ("lon", "lat"),
        scatter_dimension=0,
        tiled=True,
    )
    d_hidden_part = lax.dot_general(
        d_qkv, w_flat, (((1,), (1,)), ((), ())), preferred_element_type=jnp.float32
    )
    d_hidden = lax.psum(d_hidden_part.astype(jnp.bfloat16), "tp").astype(jnp.float32)
    attn_gain_part = jnp.sum(d_hidden * normed, 0)
    branch = norm_back(d_hidden, attn_gain, normed, inverse).astype(jnp.bfloat16)
    branch_grid = roll_out(branch.reshape(levels, lat_rows, lon_cols, features), half_lat, half_lon)
    latent_grad = (d_fine + branch_grid.astype(jnp.float32)).astype(jnp.bfloat16)
    attn_gain_grad, merge_gain_grad, rel_bias_grad = lax.psum(
        (attn_gain_part, merge_gain_part, bias_part), ("lon", "lat")
    )
    return (
        latent_grad,
        attn_gain_grad,
        qkv_weight_grad,
        proj_weight_grad,
        rel_bias_grad,
        merge_gain_grad,
        merge_weight_grad,
    )


def solution(mesh):
    placed = (
        P(None, "lat", "lon", None),
        P(),
        P(),
        P(None, None, "tp"),
        P("tp", None),
        P("tp", None),
        P(),
        P(None, "tp"),
        P(None, "lat", "lon", "tp"),
    )
    return jax.shard_map(
        local,
        mesh=mesh,
        in_specs=placed,
        out_specs=(
            P(None, "lat", "lon", None),
            P(),
            P(("lon", "lat"), None, "tp"),
            P("tp", ("lon", "lat")),
            P("tp", None),
            P(),
            P(("lon", "lat"), "tp"),
        ),
        check_vma=False,
    )
```

profile of v0, /device:TPU:2, one launch (start us, length us, event | category | flops | bytes accessed | tf_op | source)
XLA Modules:
  0.0 1943.1 jit_solution(6670305150371715838)
XLA Ops:
  7.2 1.7 slice.57
  10.4 38.7 %gather_fusion = f32[20736,4]{1,0:T(8,128)} fusion(f32[4,759]{0,1:T(8,128)S(1)} %copy.106, s32[21504]{0:T(1024)S(1)} %pad_clamp_fusion), kind=kCustom, calls=%fused_computation | custom fusion | bytes 746496 | tf_op jit(solution)/shard_map/jit(_take)/gather | solution.py:115
  49.1 8.4 copy.107
  59.2 2.3 copy.100
  64.9 6.1 collective-permute-done.1
  74.1 1.9 reshape_reshape.26
  76.0 2.0 fusion.73
  80.5 2.5 fusion.74
  83.0 2.0 fusion.10
  87.9 59.7 %all-reduce.13.cloned.1.call-done = (bf16[144,2048]{1,0:T(8,128)(2,1)}, bf16[576,512]{1,0:T(8,128)(2,1)}) async-done(((bf16[144,2048]{1,0:T(8,128)(2,1)}, bf16[576,512]{1,0:T(8,128)(2,1)}), (bf16[144,2048]{1,0:T(8,128)(2,1)}, bf16[576,512]{1,0:T(8,128)(2,1)})) %all-reduce.13.cloned.1.call-update) | async-done | bytes 1179664 | tf_op jit(solution)/shard_map/psum | solution.py:165
  147.5 2.3 bitcast_subtract_fusion
  149.8 2.8 collective-permute-start.2
  152.8 2.1 collective-permute-done.2
  154.9 1.7 collective-permute-start.3
  156.6 7.4 collective-permute-done.3
  168.3 2.3 reshape.713
  171.2 2.3 fusion.17
  175.1 2.3 reshape_reshape.29
  179.0 2.1 reshape.708
  181.2 5.2 collective-permute-done.4
  186.5 1.8 collective-permute-start.5
  188.3 5.2 collective-permute-done.5
  195.5 1.8 reshape_reshape.30
  197.3 1.9 copy.113
  199.2 2.1 reshape_reshape.31
  201.3 2.1 copy.114
  203.5 2.5 fusion.11
  211.2 4.2 copy.119
  215.3 4.1 convert_element_type.147
  219.4 2.3 copy.120
  221.8 2.2 reshape_reshape.32
  223.9 2.9 convolution_convert_fusion.2
  226.8 2.2 copy.121
  229.1 2.4 fusion.80
  231.5 3.1 fusion.79
  236.2 2.2 convert_element_type.154
  238.4 2.8 fusion.81
  241.3 28.5 %all-reduce.9.cloned.1.call-done = bf16[576,512]{1,0:T(8,128)(2,1)} async-done(((bf16[576,512]{1,0:T(8,128)(2,1)}), bf16[576,512]{1,0:T(8,128)(2,1)}) %all-reduce.9.cloned.1.call-update) | async-done | bytes 589840 | tf_op jit(solution)/shard_map/psum | solution.py:226
  269.9 1.9 fusion.22
  272.3 2.8 collective-permute-start.6
  275.2 2.1 collective-permute-done.6
  278.1 1.7 collective-permute-start.7
  282.0 5.9 copy.124
  287.9 112.5 %scatter_custom_fusion = f32[759,4]{1,0:T(8,128)S(1)} fusion(s32[20736]{0:T(1024)S(1)} %reshape.729, f32[20736,4]{1,0:T(8,128)} %copy.124, f32[]{:T(128)} %constant.95.clone.1), kind=kCustom, calls=%fused_computation.98 | custom fusion | flops 82944 | bytes 12656 | tf_op jit(solution)/shard_map/scatter-add | solution.py:197
  400.4 549.7 %all-reduce.2 = (f32[512]{0:T(512)}, f32[4,759]{0,1:T(8,128)S(1)}, f32[2048]{0:T(1024)}) all-reduce(f32[512]{0:T(512)S(1)} %get-tuple-element.45, f32[4,759]{0,1:T(8,128)S(1)} %bitcast.144, f32[2048]{0:T(1024)S(1)} %copy-done.24), channel_id=1, replica_groups=mesh['lon'=16,'lat'=8,'tp'=2] {'lon','lat'}, use_global_device_ids=true, to_apply=%region_16.17 | all-reduce | flops 5596 | bytes 44768 | tf_op jit(solution)/shard_map/psum | solution.py:231
  950.9 2.2 add_convert_fusion
  953.1 415.8 %all-reduce.11.cloned.1.call-done = (f32[512,3,256]{2,0,1:T(8,128)}, f32[256,512]{0,1:T(8,128)}) async-done(((f32[512,3,256]{2,0,1:T(8,128)}, f32[256,512]{0,1:T(8,128)}), (f32[512,3,256]{2,0,1:T(8,128)}, f32[256,512]{0,1:T(8,128)})) %all-reduce.11.cloned.1.call-update) | async-done | bytes 2097168
  1371.6 564.5 %reduce-scatter.3.cloned.1.call-done = f32[16,512]{1,0:T(8,128)} async-done(((f32[2048,512]{1,0:T(8,128)}), f32[16,512]{1,0:T(8,128)}) %reduce-scatter.3.cloned.1.call-update) | async-done | bytes 32784 | tf_op jit(solution)/shard_map/reduce_scatter | solution.py:167
  (157 shorter events, 38.4 us)
Async XLA Ops:
  7.2 56.1 %copy-start = (bf16[2048,512]{1,0:T(8,128)(2,1)S(1)}, bf16[2048,512]{1,0:T(8,128)(2,1)}, u32[]{:S(2)}) copy-start(bf16[2048,512]{1,0:T(8,128)(2,1)} %param.16) | copy-start | bytes 6291460
  7.2 140.3 %all-reduce.13.cloned.1.call-start = ((), (), s32[]{:S(2)}) async-start(), calls=%async_computation.4 | async-start | bytes 2359296 | tf_op jit(solution)/shard_map/psum | solution.py:165
  8.9 52.6 %collective-permute-start = (bf16[2,6,6,512]{3,2,1,0:T(8,128)(2,1)}, bf16[2,6,6,512]{3,2,1,0:T(8,128)(2,1)S(1)}, u32[]{:S(2)}, u32[]{:S(2)}) collective-permute-start(bf16[2,6,6,512]{3,2,1,0:T(8,128)(2,1)} %slice.57), channel_id=1, source_target_pairs={{240,0},{0,16},{16,32},{32,48},{48,64},{64,80},{80,96},{96,112},{1... | collective-permute-start | bytes 221192 | tf_op jit(solution)/shard_map/ppermute | solution.py:17
  49.1 8.5 copy-start.30
  58.1 3.4 copy-start.5
  59.2 4.1 copy-start.17
  61.6 9.4 collective-permute-start.1
  64.9 6.7 copy-start.25
  71.3 1.5 copy-start.16
  71.9 0.8 copy-start.9
  79.3 1.2 copy-start.19
  79.9 3.1 copy-start.11
  80.5 2.5 copy-start.13
  80.5 2.5 copy-start.20
  83.0 2.0 copy-start.26
  85.6 1.0 copy-start.15
  87.7 182.1 %all-reduce.9.cloned.1.call-start = ((), (), s32[]{:S(2)}) async-start(), calls=%async_computation.1 | async-start | bytes 1179648 | tf_op jit(solution)/shard_map/psum | solution.py:226
  149.8 5.0 collective-permute-start.2
  154.9 9.1 collective-permute-start.3
  168.2 3.0 copy-start.23
  170.6 3.0 copy-start.28
  171.2 2.3 copy-start.8
  171.2 2.3 copy-start.29
  181.2 5.3 collective-permute-start.4
  186.5 7.0 collective-permute-start.5
  193.6 0.8 copy-start.2
  197.3 6.1 copy-start.27
  203.5 2.5 copy-start.7
  203.5 2.6 copy-start.21
  203.5 2.8 copy-start.22
  206.8 1.5 copy-start.14
  208.3 1.0 copy-start.12
  226.8 1142.2 %all-reduce.11.cloned.1.call-start = ((), (), s32[]{:S(2)}) async-start(), calls=%async_computation.3 | async-start | bytes 4194304
  229.1 2.4 copy-start.4
  234.5 1701.6 %reduce-scatter.3.cloned.1.call-start = ((), (), s32[]{:S(2)}) async-start(), calls=%async_computation.2 | async-start | bytes 4227072 | tf_op jit(solution)/shard_map/reduce_scatter | solution.py:167
  234.6 3.8 copy-start.18
  241.2 28.6 %copy-start.3 = (f32[576,512]{1,0:T(8,128)S(1)}, f32[576,512]{1,0:T(8,128)}, u32[]{:S(2)}) copy-start(f32[576,512]{1,0:T(8,128)} %get-tuple-element.66) | copy-start | bytes 3538948
  269.8 1.9 copy-start.10
  272.3 7.7 copy-start.31
  272.3 9.0 copy-start.6
  272.3 5.0 collective-permute-start.6
  278.1 672.9 %collective-permute-start.7 = (bf16[2,3,48,512]{3,2,1,0:T(8,128)(2,1)S(1)}, bf16[2,3,48,512]{3,2,1,0:T(8,128)(2,1)}, u32[]{:S(2)}, u32[]{:S(2)}) collective-permute-start(bf16[2,3,48,512]{3,2,1,0:T(8,128)(2,1)S(1)} %get-tuple-element.63), channel_id=1, source_target_pairs={{2,0},{4,2},{6,4},{8,6},{10,8},{12,10},{14,12},{0,14},{3,1},{5,3},... | collective-permute-start | bytes 884744 | tf_op jit(solution)/shard_map/ppermute | solution.py:17
  282.0 118.4 %copy-start.24 = (f32[2048]{0:T(1024)S(1)}, f32[2048]{0:T(1024)}, u32[]{:S(2)}) copy-start(f32[2048]{0:T(1024)} %get-tuple-element.42) | copy-start | bytes 24580
  950.9 985.2 %copy-start.1 = (bf16[2048,512]{1,0:T(8,128)(2,1)S(1)}, bf16[2048,512]{1,0:T(8,128)(2,1)}, u32[]{:S(2)}) copy-start(bf16[2048,512]{1,0:T(8,128)(2,1)} %param.16) | copy-start | bytes 6291460
Sparse Core Ops, SparseCore 0:
  87.9 59.6 all-reduce.12
  226.9 42.8 all-reduce.8
  272.5 1096.3 all-reduce.10
  1372.0 564.0 reduce-scatter.2
where the time goes:
time: 1960 us; the launch traced here: 1940 us
  waiting for transfers between devices  1100 us (56%)
  blocking collectives  550 us (28%)
  other arithmetic  133 us (7%)
  local copies, waits for them, and re-layouts  112 us (6%)
  matrix products  24.1 us (1%)
    reduce_scatter x1, waiting for transfers between devices, local(): lax.psum_scatter(lax.dot_general(columns, coarse_flat, (((0,), (0,)), (()...  565 us
    psum x1, blocking collectives, local(): lax.psum((attn_gain_part, merge_gain_part, bias_part), ('lon', 'lat'))  550 us
    unnamed x5, waiting for transfers between devices  416 us
    scatter-add x1, other arithmetic, local(): jax.ops.segment_sum(score_total.T, rel.reshape(-1), rel_bias.shape[1])  113 us
    psum x1, waiting for transfers between devices, local(): lax.psum(d_partial.astype(jnp.bfloat16), 'tp').astype(jnp.float32)  59.7 us
    gather x2, local copies, waits for them, and re-layouts, local(): bias_block = jnp.take(rel_bias, rel, axis=1)  47.1 us
  transfers between devices with their start and end apart: 12, of which 10 were waited for; matrix products, arithmetic and copies ran while one was open for 10% of the time, Pallas kernels for 0%

commit v1 on v0

v1 whole, which is shorter than its diff:
```python
import functools

import jax
import jax.numpy as jnp
import numpy as np
from jax import lax
from jax.experimental import pallas as pl
from jax.experimental.pallas import tpu as pltpu
from jax.sharding import PartitionSpec as P

EPS = 1e-05
NEG = -1e30
MESH = pl.DeviceIdType.MESH
BF = jnp.bfloat16
F32 = jnp.float32

LEV, ROWS, COLS, D = 2, 6, 48, 512
WLON = 12
NWIN = COLS // WLON
WTOK = LEV * ROWS * WLON
TOK = LEV * ROWS * COLS
HEADS = 4
HD = 64
DA = HEADS * HD
NREL = 759
NZ, NY = 8, 4


def onehot(rows, cols, pairs):
    out = np.zeros((rows, cols), np.float32)
    for r, c in pairs:
        out[r, c] = 1.0
    return out.astype(jnp.bfloat16)


def piece_lists(row_sets, pads):
    own_rows, next_rows = row_sets
    near, far = range(0, 42), range(42, 48)
    out, base = [], 0
    for (rows, cols), pad in zip(
        ((own_rows, near), (own_rows, far), (next_rows, near), (next_rows, far)), pads
    ):
        items = [(l, r, c) for l in range(LEV) for r in rows for c in cols]
        out.append([(base + n, it) for n, it in enumerate(items)])
        base += pad
    return out, base


@functools.lru_cache(None)
def tables():
    t = {}
    pieces, total = piece_lists((range(0, 4), range(2, 6)), (336, 48, 336, 48))
    t["Ql"] = onehot(
        total, TOK, [(p, (l * ROWS + r) * COLS + c) for pc in pieces for p, (l, r, c) in pc]
    )
    where = {}
    for n, pc in enumerate(pieces):
        for p, (l, r, c) in pc:
            rr = r + 4 if n < 2 else r - 2
            sc = c + 6 if n % 2 == 0 else c - 42
            where[(l, rr, sc)] = p

    def merge_at(l, rr, sc):
        return ((rr * 2 + sc % 2) * LEV + l) * 24 + sc // 2

    def window_at(l, rr, sc):
        return (sc // WLON) * WTOK + (l * ROWS + rr - 1) * WLON + sc % WLON

    band = [(l, rr, sc) for l in range(LEV) for rr in range(8) for sc in range(COLS)]
    inner = [k for k in band if 1 <= k[1] <= 6]
    t["PxM"] = onehot(768, total, [(merge_at(*k), where[k]) for k in band])
    t["Pxw"] = onehot(TOK, total, [(window_at(*k), where[k]) for k in inner])
    t["PwM"] = onehot(TOK, TOK, [(merge_at(*k) - 96, window_at(*k)) for k in inner])
    t["PMw"] = np.ascontiguousarray(t["PwM"].T)
    pads = (256, 48, 256, 48)
    pieces, total = piece_lists((range(0, 3), range(3, 6)), pads)
    out, back = [], []
    for n, pc in enumerate(pieces):
        for p, (l, r, c) in pc:
            rr = r + 4 if n < 2 else r - 2
            sc = c + 6 if n % 2 == 0 else c - 42
            out.append((p, window_at(l, rr, sc)))
            back.append(((l * ROWS + r) * COLS + c, p))
    t["Ppo"] = onehot(total, TOK, out)
    t["Pf"] = onehot(TOK, total, back)
    base, cpairs, cwhere = 0, [], {}
    for n, (rows, cols, pad) in enumerate(
        (
            ((0, 1), range(0, 21), 96),
            ((0, 1), range(21, 24), 16),
            ((1, 2), range(0, 21), 96),
            ((1, 2), range(21, 24), 16),
        )
    ):
        p = base
        for l in range(LEV):
            for r in rows:
                for c in cols:
                    cpairs.append((p, (l * 3 + r) * 24 + c))
                    cr = r + 2 if n < 2 else r - 1
                    cc = c + 3 if n % 2 == 0 else c - 21
                    cwhere[(cr, l, cc)] = p
                    p += 1
        base += pad
    t["Qc"] = onehot(base, 144, cpairs)
    t["Pc"] = onehot(
        192, base, [((cr * LEV + l) * 24 + cc, p) for (cr, l, cc), p in cwhere.items()]
    )
    ep = []
    for c in range(WLON):
        for j in range(WTOK):
            l2, r2, c2 = j // 72, j // 12 % 6, j % 12
            ep.append((c * WTOK + j, ((1 - l2) * 11 + 5 - r2) * 23 + c - c2 + 11))
    t["E"] = onehot(WLON * WTOK, 512, ep)
    return t


def mm(a, b):
    return lax.dot_general(a, b, (((1,), (0,)), ((), ())), preferred_element_type=F32)


def mm_nt(a, b):
    return lax.dot_general(a, b, (((1,), (1,)), ((), ())), preferred_element_type=F32)


def mm_tn(a, b):
    return lax.dot_general(a, b, (((0,), (0,)), ((), ())), preferred_element_type=F32)


def layer_stats(x):
    center = x - jnp.mean(x, -1, keepdims=True)
    inverse = lax.rsqrt(jnp.mean(center * center, -1, keepdims=True) + EPS)
    return center * inverse, inverse


def norm_back(up, gain, normed, inverse):
    s = up * gain
    return inverse * (
        s - jnp.mean(s, -1, keepdims=True) - normed * jnp.mean(s * normed, -1, keepdims=True)
    )


def head_mask(h, rows):
    lane = lax.broadcasted_iota(jnp.int32, (rows, DA), 1)
    return (lane >= h * HD) & (lane < (h + 1) * HD)


def stack_heads(x):
    zero = jnp.zeros_like(x)
    return jnp.concatenate(
        [jnp.where(head_mask(h, x.shape[0]), x, zero) for h in range(HEADS)], 0
    )


def vspec():
    return pl.BlockSpec(memory_space=pltpu.VMEM)


def call(kernel, name, ins, outs, scratch=(), cid=None, smem=0, flops=10**9):
    params = dict(vmem_limit_bytes=56 << 20)
    if cid is not None:
        params.update(collective_id=cid, has_side_effects=True)
    specs = [pl.BlockSpec(memory_space=pltpu.SMEM)] * smem + [vspec()] * (len(ins) - smem)
    return pl.pallas_call(
        kernel,
        out_shape=[jax.ShapeDtypeStruct(s, d) for s, d in outs],
        in_specs=specs,
        out_specs=[vspec()] * len(outs),
        scratch_shapes=list(scratch),
        compiler_params=pltpu.CompilerParams(**params),
        cost_estimate=pl.CostEstimate(flops=flops, bytes_accessed=8 << 20, transcendentals=0),
        name=name,
    )(*ins)


def device(dlon, dlat, dtp):
    nlon, nlat = lax.axis_size("lon"), lax.axis_size("lat")
    return (
        lax.rem(lax.axis_index("lon") + dlon + nlon, nlon),
        lax.rem(lax.axis_index("lat") + dlat + nlat, nlat),
        lax.rem(lax.axis_index("tp") + dtp, 2),
    )


def greet(partners):
    barrier = pltpu.get_barrier_semaphore()
    for d in partners:
        pl.semaphore_signal(barrier, inc=1, device_id=d, device_id_type=MESH)
    pl.semaphore_wait(barrier, len(partners))


def remote(src, dst, ss, rs, n, dev):
    return pltpu.make_async_remote_copy(
        src, dst, ss.at[n], rs.at[n], device_id=dev, device_id_type=MESH
    )


def kin(lat_ref, cg_ref, ql_ref, qc_ref, pc_ref, cc_ref, sp, sc, ss, rs):
    greet([device(s * o, s * a, 0) for s in (1, -1) for o, a in ((1, 0), (0, 1), (1, 1))])
    copies = []

    def send(n, lo, hi, clo, chi, dev):
        sp[lo:hi, :] = mm(ql_ref[lo:hi, :], lat_ref[...]).astype(BF)
        c = remote(sp.at[lo:hi], pc_ref.at[lo:hi], ss, rs, 2 * n, dev)
        c.start()
        sc[clo:chi, :] = mm(qc_ref[clo:chi, :], cg_ref[...]).astype(BF)
        k = remote(sc.at[clo:chi], cc_ref.at[clo:chi], ss, rs, 2 * n + 1, dev)
        k.start()
        copies.extend([c, k])

    send(0, 384, 720, 112, 208, device(0, 1, 0))
    send(1, 720, 768, 208, 224, device(1, 1, 0))
    send(2, 336, 384, 96, 112, device(1, 0, 0))
    pc_ref[0:336, :] = mm(ql_ref[0:336, :], lat_ref[...]).astype(BF)
    cc_ref[0:96, :] = mm(qc_ref[0:96, :], cg_ref[...]).astype(BF)
    for c in copies:
        c.wait()


def kdm(cc_ref, pc_ref, mw_ref, cm_ref, dm_ref):
    cm_ref[...] = mm(pc_ref[...], cc_ref[...]).astype(BF)
    for n in range(4):
        cols = slice(n * 512, (n + 1) * 512)
        dm_ref[:, cols] = mm_nt(cm_ref[...], mw_ref[cols, :]).astype(BF)


def kfwd(
    pole_ref, pc_ref, gain_ref, w_ref, proj_ref, tab_ref, e_ref, pxw_ref, pwm_ref,
    z_ref, qkv_ref, p_ref, hn_ref, ao_ref, bm, u, wide,
):
    for l in range(LEV):
        for r in range(ROWS):
            shift = (l * 11 + r) * 23
            row = tab_ref[...]
            if shift:
                row = pltpu.roll(row, 768 - shift, 1)
            for h in range(HEADS):
                n = h * 12 + l * ROWS + r
                u[n : n + 1, :] = row[h : h + 1, :512]
    t0 = u[...]
    hi = t0.astype(BF)
    rest = t0 - hi.astype(F32)
    mid = rest.astype(BF)
    low = (rest - mid.astype(F32)).astype(BF)
    split = jnp.concatenate([hi, mid, low], 0)
    for c in range(WLON):
        y = mm_nt(split, e_ref[c * WTOK : (c + 1) * WTOK, :])
        y = y[0:48] + y[48:96] + y[96:144]
        wide[0, pl.ds(c, 48, stride=WLON), :] = y[:, 0:128]
        wide[1, pl.ds(c, 48, stride=WLON), :] = jnp.concatenate(
            [y[:, 128:WTOK], jnp.zeros((48, 256 - WTOK), F32)], 1
        )
    band = lax.axis_index("lat")
    nrows = pole_ref.shape[0]
    i = lax.broadcasted_iota(jnp.int32, (WTOK, WTOK), 0)
    j = lax.broadcasted_iota(jnp.int32, (WTOK, WTOK), 1)
    ri, rj = lax.rem(lax.div(i, WLON), ROWS), lax.rem(lax.div(j, WLON), ROWS)
    valid = jnp.zeros((WTOK, WTOK), jnp.int32)
    for r in range(ROWS):
        flag = pole_ref[lax.rem(band * ROWS + (r - 3 + nrows), nrows)]
        valid = jnp.where(rj == r, flag, valid)
    cut = jnp.where(band == 0, 3, 0)
    same = jnp.where(ri < cut, 1, 0) == jnp.where(rj < cut, 1, 0)
    allowed = (valid > 0) & same
    for h in range(HEADS):
        rows = slice(h * WTOK, (h + 1) * WTOK)
        both = jnp.concatenate([wide[0, rows, :], wide[1, rows, 0 : WTOK - 128]], 1)
        bm[rows, :] = jnp.where(allowed, both, NEG)

    normed, _ = layer_stats(mm(pxw_ref[...], pc_ref[...]))
    hn_ref[...] = (normed * gain_ref[...]).astype(BF)
    qkv_ref[...] = mm(hn_ref[...], w_ref[...]).astype(BF)

    def window(w, carry):
        rows = pl.ds(pl.multiple_of(w * WTOK, 16), WTOK)
        q = qkv_ref[rows, 0:DA]
        k = qkv_ref[rows, DA : 2 * DA]
        v = qkv_ref[rows, 2 * DA : 3 * DA]
        s = mm_nt(stack_heads(q), k) * (HD**-0.5) + bm[...]
        e = jnp.exp(s - jnp.max(s, -1, keepdims=True))
        p = e / jnp.sum(e, -1, keepdims=True)
        p_ref[w] = p
        pb = p.astype(BF)
        vs = stack_heads(v)
        o = jnp.zeros((WTOK, DA), F32)
        for h in range(HEADS):
            at = slice(h * WTOK, (h + 1) * WTOK)
            o = o + mm(pb[at], vs[at])
        ao_ref[rows, :] = o.astype(BF)
        return carry

    lax.fori_loop(0, NWIN, window, 0)
    z_ref[...] = mm(mm(pwm_ref[...], ao_ref[...]).astype(BF), proj_ref[...]).astype(BF)


def kyx(z_ref, zp_ref, zh_ref, ss, rs):
    greet([device(0, 0, 1)] + [device(0, a, t) for a in (1, -1) for t in (0, 1)])
    copies = [
        remote(z_ref.at[480:576], zh_ref.at[0], ss, rs, 0, device(0, 1, 0)),
        remote(z_ref.at[480:576], zh_ref.at[1], ss, rs, 1, device(0, 1, 1)),
        remote(z_ref.at[0:96], zh_ref.at[2], ss, rs, 2, device(0, -1, 0)),
        remote(z_ref.at[0:96], zh_ref.at[3], ss, rs, 3, device(0, -1, 1)),
        remote(z_ref, zp_ref, ss, rs, 4, device(0, 0, 1)),
    ]
    for c in copies:
        c.start()
    for c in copies:
        c.wait()


def kmerge(
    pc_ref, pxm_ref, z_ref, zp_ref, zh_ref, dmo_ref, dmp_ref, cm_ref, gain_ref,
    dy_ref, gm_ref, mg_ref, y, mb,
):
    def total(lo, hi, a, b):
        x = mm(pxm_ref[lo:hi, :], pc_ref[...])
        y[lo:hi, :] = (x + (a.astype(F32) + b.astype(F32))).astype(BF)

    total(0, 96, zh_ref[0], zh_ref[1])
    total(96, 672, z_ref[...], zp_ref[...])
    total(672, 768, zh_ref[2], zh_ref[3])
    gain = gain_ref[...]
    acc = jnp.zeros((1, 4 * D), F32)
    for cr in range(4):
        slabs = [
            y[(2 * cr + rp) * 96 + cp * 48 : (2 * cr + rp) * 96 + cp * 48 + 48, :]
            for rp in (0, 1)
            for cp in (0, 1)
        ]
        hat, inv = layer_stats(jnp.concatenate(slabs, 1).astype(F32))
        at = slice(cr * 48, (cr + 1) * 48)
        dm = dmo_ref[at, :].astype(F32) + dmp_ref[at, :].astype(F32)
        if cr > 0:
            acc = acc + jnp.sum(dm * hat, 0, keepdims=True)
            mb[(cr - 1) * 48 : cr * 48, :] = (hat * gain).astype(BF)
        dy = norm_back(dm, gain, hat, inv).astype(BF)
        for q in range(4):
            r = 2 * cr + q // 2
            if 1 <= r <= 6:
                lo = (r - 1) * 96 + (q % 2) * 48
                dy_ref[lo : lo + 48, :] = dy[:, q * D : (q + 1) * D]
    mg_ref[...] = acc
    for n in range(4):
        at = slice(n * 512, (n + 1) * 512)
        gm_ref[at, :] = mm_tn(mb[:, at], cm_ref[48:192, :])


def kbwd(
    dy_ref, pmw_ref, proj_ref, w_ref, qkv_ref, p_ref, hn_ref, ao_ref, e_ref, ppo_ref,
    dhp_ref, dyp_ref, gq_ref, bias_ref, dyw, do, dqkv, dst, t, wide,
):
    scale = HD**-0.5
    dyw[...] = mm(pmw_ref[...], dy_ref[...]).astype(BF)
    do[...] = mm_nt(dyw[...], proj_ref[...]).astype(BF)
    dst[...] = jnp.zeros_like(dst)

    def window(w, carry):
        rows = pl.ds(pl.multiple_of(w * WTOK, 16), WTOK)
        q = qkv_ref[rows, 0:DA]
        k = qkv_ref[rows, DA : 2 * DA]
        v = qkv_ref[rows, 2 * DA : 3 * DA]
        p = p_ref[w]
        dos = stack_heads(do[rows, :])
        dp = mm_nt(dos, v)
        dv = mm_tn(p.astype(BF), dos)
        ds = p * (dp - jnp.sum(dp * p, -1, keepdims=True))
        dst[...] = dst[...] + ds
        dsb = ds.astype(BF)
        dk = mm_tn(dsb, stack_heads(q)) * scale
        ks = stack_heads(k)
        dq = jnp.zeros((WTOK, DA), F32)
        for h in range(HEADS):
            at = slice(h * WTOK, (h + 1) * WTOK)
            dq = dq + mm(dsb[at], ks[at])
        dqkv[rows, 0:DA] = (dq * scale).astype(BF)
        dqkv[rows, DA : 2 * DA] = dk.astype(BF)
        dqkv[rows, 2 * DA : 3 * DA] = dv.astype(BF)
        return carry

    lax.fori_loop(0, NWIN, window, 0)
    dh = mm_nt(dqkv[...], w_ref[...]).astype(BF)
    dhp_ref[...] = mm(ppo_ref[...], dh).astype(BF)
    dyp_ref[...] = mm(ppo_ref[...], dyw[...]).astype(BF)
    gq_ref[:, 0 : 3 * DA] = mm_tn(hn_ref[...], dqkv[...])
    gq_ref[:, 3 * DA :] = mm_tn(dyw[...], ao_ref[...])
    acc = jnp.zeros((48, 512), F32)
    wide[0] = dst[:, 0:128]
    wide[1, :, 0 : WTOK - 128] = dst[:, 128:WTOK]
    for c in range(WLON):
        rows = pl.ds(c, 48, stride=WLON)
        x = jnp.concatenate([wide[0, rows, :], wide[1, rows, :][:, 0 : WTOK - 128]], 1)
        hi = x.astype(BF)
        low = (x - hi.astype(F32)).astype(BF)
        y = mm(jnp.concatenate([hi, low], 0), e_ref[c * WTOK : (c + 1) * WTOK, :])
        acc = acc + y[0:48] + y[48:96]
    t[:, 0:512] = acc
    t[:, 512:768] = jnp.zeros((48, 256), F32)
    for h in range(HEADS):
        out = jnp.zeros((1, 768), F32)
        for g in range(12):
            row = t[h * 12 + g : h * 12 + g + 1, :]
            shift = (g // ROWS * 11 + g % ROWS) * 23
            out = out + (pltpu.roll(row, shift, 1) if shift else row)
        bias_ref[h : h + 1, :] = out


OUT = ((0, 256), (256, 304), (304, 560), (560, 608))
OUT_TO = ((0, 0), (-1, 0), (0, -1), (-1, -1))


def kout(dh_ref, dy_ref, dhr_ref, dyr_ref, ss, rs):
    greet(
        [device(0, 0, 1)]
        + [device(s * o, s * a, t) for s in (1, -1) for o, a in OUT_TO[1:] for t in (0, 1)]
    )
    copies = []
    for n in (2, 0, 3, 1):
        lo, hi = OUT[n]
        o, a = OUT_TO[n]
        at = slice(lo, hi)
        copies.append(
            remote(dh_ref.at[at], dhr_ref.at[1, at], ss, rs, n, device(o, a, 1))
        )
        if n:
            copies.append(
                remote(dh_ref.at[at], dhr_ref.at[0, at], ss, rs, 4 + n, device(o, a, 0))
            )
            copies.append(remote(dy_ref.at[at], dyr_ref.at[at], ss, rs, 8 + n, device(o, a, 0)))
    for c in copies:
        c.start()
    dhr_ref[0, 0:256, :] = dh_ref[0:256, :]
    dyr_ref[0:256, :] = dy_ref[0:256, :]
    for c in copies:
        c.wait()


def kfin(lat_ref, gain_ref, pf_ref, dhr_ref, dyr_ref, lg_ref, ag_ref):
    pf = pf_ref[...]
    normed, inv = layer_stats(lat_ref[...].astype(F32))
    dh = mm(pf, dhr_ref[0]) + mm(pf, dhr_ref[1])
    ag_ref[...] = jnp.sum(dh * normed, 0, keepdims=True)
    branch = norm_back(dh, gain_ref[...], normed, inv).astype(BF)
    lg_ref[...] = (mm(pf, dyr_ref[...]) + branch.astype(F32)).astype(BF)


def krs(
    gm_ref, gq_ref, sv_ref, om_ref, oq_ref, ov_ref,
    sm1, sq1, rm1, rq1, sv1,
    am, aq, sm2, sq2, rm2, rq2, sv2,
    bmm, bq, sm3, rm3, rq3, sv3,
    cm, cq, rm4, rq4, sv4, ss, rs,
):
    lon, lat, tp = lax.axis_index("lon"), lax.axis_index("lat"), lax.axis_index("tp")
    z, core = lax.div(lon, 2), lax.rem(lon, 2)
    yy, xx = lax.div(lat, 2), lax.rem(lat, 2)
    core_dev = (z * 2 + 1 - core, lat, tp)
    x_dev = (lon, yy * 2 + 1 - xx, tp)
    y_devs = [(lon, lax.rem(yy + k, NY) * 2 + xx, tp) for k in range(1, NY)]
    z_devs = [(lax.rem(z + k, NZ) * 2 + core, lat, tp) for k in range(1, NZ)]
    greet([core_dev, x_dev] + y_devs + z_devs)

    for iy in range(NY):
        for iz in range(NZ):
            sm1[iy, iz] = gm_ref[iz, 1 - core, iy].astype(BF)
        for iz in range(0, NZ, 2):
            pair = jnp.concatenate([gq_ref[iz, 1 - core, iy], gq_ref[iz + 1, 1 - core, iy]], 0)
            sq1[iy, iz * 8 : iz * 8 + 16, :] = pair.astype(BF)
    sv1[core] = sv_ref[...]
    copies = [
        remote(sm1, rm1, ss, rs, 0, core_dev),
        remote(sq1, rq1, ss, rs, 1, core_dev),
        remote(sv1.at[core], sv1.at[core], ss, rs, 2, core_dev),
    ]
    for c in copies:
        c.start()
    for c in copies:
        c.wait()
    sv2[yy] = sv1[0] + sv1[1]

    copies = []
    for k in range(1, NY):
        iy = lax.rem(yy + k, NY)
        for iz in range(NZ):
            sm2[k - 1, iz] = (gm_ref[iz, core, iy] + rm1[iy, iz].astype(F32)).astype(BF)
        for iz in range(0, NZ, 2):
            pair = jnp.concatenate([gq_ref[iz, core, iy], gq_ref[iz + 1, core, iy]], 0)
            at = slice(iz * 8, iz * 8 + 16)
            sq2[k - 1, at, :] = (pair + rq1[iy, at, :].astype(F32)).astype(BF)
        n = 3 * k
        for c in (
            remote(sm2.at[k - 1], rm2.at[k - 1], ss, rs, n, y_devs[k - 1]),
            remote(sq2.at[k - 1], rq2.at[k - 1], ss, rs, n + 1, y_devs[k - 1]),
            remote(sv2.at[yy], sv2.at[yy], ss, rs, n + 2, y_devs[k - 1]),
        ):
            c.start()
            copies.append(c)
    for iz in range(NZ):
        am[iz] = gm_ref[iz, core, yy] + rm1[yy, iz].astype(F32)
    for iz in range(0, NZ, 2):
        pair = jnp.concatenate([gq_ref[iz, core, yy], gq_ref[iz + 1, core, yy]], 0)
        at = slice(iz * 8, iz * 8 + 16)
        aq[at, :] = pair + rq1[yy, at, :].astype(F32)
    for c in copies:
        c.wait()
    sv3[z] = sv2[0] + sv2[1] + sv2[2] + sv2[3]
    for iz in range(NZ):
        acc = am[iz]
        for k in range(NY - 1):
            acc = acc + rm2[k, iz].astype(F32)
        bmm[iz] = acc
    acc = aq[...]
    for k in range(NY - 1):
        acc = acc + rq2[k].astype(F32)
    for iz in range(NZ):
        bq[iz] = acc[iz * 8 : iz * 8 + 8]

    copies = []
    for k in range(1, NZ):
        iz = lax.rem(z + k, NZ)
        sm3[k - 1] = bmm[iz].astype(BF)
        n = 9 + 3 * k
        for c in (
            remote(sm3.at[k - 1], rm3.at[k - 1], ss, rs, n, z_devs[k - 1]),
            remote(bq.at[iz], rq3.at[k - 1], ss, rs, n + 1, z_devs[k - 1]),
            remote(sv3.at[z], sv3.at[z], ss, rs, n + 2, z_devs[k - 1]),
        ):
            c.start()
            copies.append(c)
    for c in copies:
        c.wait()
    acc = sv3[0]
    for k in range(1, NZ):
        acc = acc + sv3[k]
    sv4[xx] = acc
    acc, accq = bmm[z], bq[z]
    for k in range(NZ - 1):
        acc = acc + rm3[k].astype(F32)
        accq = accq + rq3[k]
    cm[0] = acc[0:16]
    cm[1] = acc[16:32]
    cq[...] = accq

    copies = [
        remote(cm.at[1 - xx], rm4, ss, rs, 33, x_dev),
        remote(cq, rq4, ss, rs, 34, x_dev),
        remote(sv4.at[xx], sv4.at[xx], ss, rs, 35, x_dev),
    ]
    for c in copies:
        c.start()
    for c in copies:
        c.wait()
    om_ref[...] = cm[xx] + rm4[...]
    both = cq[...] + rq4[...]
    oq_ref[...] = jnp.where(xx == 0, both[0:4], both[4:8])
    ov_ref[...] = sv4[0] + sv4[1]


def reduce_weights(gm, gq, sv):
    nv = sv.shape
    scratch = [
        pltpu.VMEM((NY, NZ, 32, 512), BF), pltpu.VMEM((NY, 64, 1024), BF),
        pltpu.VMEM((NY, NZ, 32, 512), BF), pltpu.VMEM((NY, 64, 1024), BF),
        pltpu.VMEM((2,) + nv, F32),
        pltpu.VMEM((NZ, 32, 512), F32), pltpu.VMEM((64, 1024), F32),
        pltpu.VMEM((NY - 1, NZ, 32, 512), BF), pltpu.VMEM((NY - 1, 64, 1024), BF),
        pltpu.VMEM((NY - 1, NZ, 32, 512), BF), pltpu.VMEM((NY - 1, 64, 1024), BF),
        pltpu.VMEM((NY,) + nv, F32),
        pltpu.VMEM((NZ, 32, 512), F32), pltpu.VMEM((NZ, 8, 1024), F32),
        pltpu.VMEM((NZ - 1, 32, 512), BF), pltpu.VMEM((NZ - 1, 32, 512), BF),
        pltpu.VMEM((NZ - 1, 8, 1024), F32), pltpu.VMEM((NZ,) + nv, F32),
        pltpu.VMEM((2, 16, 512), F32), pltpu.VMEM((8, 1024), F32),
        pltpu.VMEM((16, 512), F32), pltpu.VMEM((8, 1024), F32), pltpu.VMEM((2,) + nv, F32),
        pltpu.SemaphoreType.DMA((36,)), pltpu.SemaphoreType.DMA((36,)),
    ]
    return call(
        krs, "weight_sums",
        [gm.reshape(NZ, 2, NY, 32, 512), gq.reshape(NZ, 2, NY, 8, 1024), sv],
        [((16, 512), F32), ((4, 1024), F32), (nv, F32)],
        scratch, cid=4,
    )


def local(
    latent, pole_mask, attn_gain, qkv_weight, proj_weight, rel_bias, merge_gain, merge_weight,
    coarse_grad,
):
    t = {k: jnp.asarray(v) for k, v in tables().items()}
    dma = pltpu.SemaphoreType.DMA
    lat = latent.reshape(TOK, D)
    w = qkv_weight.reshape(D, 3 * DA)
    gain = attn_gain.reshape(1, D)
    tab = jnp.pad(rel_bias, ((0, 0), (0, 768 - NREL)))

    pc, cc = call(
        kin, "way_in", [lat, coarse_grad.reshape(144, 512), t["Ql"], t["Qc"]],
        [((768, D), BF), ((224, 512), BF)],
        [pltpu.VMEM((768, D), BF), pltpu.VMEM((224, 512), BF), dma((6,)), dma((6,))], cid=1,
    )
    cm, dmo = call(
        kdm, "coarse_cotangent", [cc, t["Pc"], merge_weight],
        [((192, 512), BF), ((192, 4 * D), BF)],
    )
    dmp = lax.ppermute(dmo, "tp", [(0, 1), (1, 0)])
    z, qkv, p, hn, ao = call(
        kfwd, "attention_forward",
        [pole_mask, pc, gain, w, proj_weight, tab, t["E"], t["Pxw"], t["PwM"]],
        [
            ((TOK, D), BF), ((TOK, 3 * DA), BF), ((NWIN, HEADS * WTOK, WTOK), F32),
            ((TOK, D), BF), ((TOK, DA), BF),
        ],
        [
            pltpu.VMEM((HEADS * WTOK, WTOK), F32), pltpu.VMEM((48, 512), F32),
            pltpu.VMEM((2, HEADS * WTOK, 128), F32),
        ],
        smem=1, flops=4 * 10**9,
    )
    zp, zh = call(
        kyx, "attention_sums", [z], [((TOK, D), BF), ((4, 96, D), BF)], [dma((5,)), dma((5,))],
        cid=2,
    )
    dy, gm, mg = call(
        kmerge, "patch_merge",
        [pc, t["PxM"], z, zp, zh, dmo, dmp, cm, merge_gain.reshape(1, 4 * D)],
        [((TOK, D), BF), ((4 * D, 512), F32), ((1, 4 * D), F32)],
        [pltpu.VMEM((768, D), BF), pltpu.VMEM((144, 4 * D), BF)],
    )
    dhp, dyp, gq, bias = call(
        kbwd, "attention_backward",
        [dy, t["PMw"], proj_weight, w, qkv, p, hn, ao, t["E"], t["Ppo"]],
        [((608, D), BF), ((608, D), BF), ((D, 1024), F32), ((HEADS, 768), F32)],
        [
            pltpu.VMEM((TOK, D), BF), pltpu.VMEM((TOK, DA), BF), pltpu.VMEM((TOK, 3 * DA), BF),
            pltpu.VMEM((HEADS * WTOK, WTOK), F32), pltpu.VMEM((48, 768), F32),
            pltpu.VMEM((2, HEADS * WTOK, 128), F32),
        ],
    )
    dhr, dyr = call(
        kout, "way_out", [dhp, dyp], [((2, 608, D), BF), ((608, D), BF)], [dma((12,)), dma((12,))],
        cid=3,
    )
    lg, ag = call(
        kfin, "latent_cotangent", [lat, gain, t["Pf"], dhr, dyr],
        [((TOK, D), BF), ((1, D), F32)],
    )
    sv = jnp.concatenate([ag, mg, bias.reshape(1, HEADS * 768)], 1).reshape(44, 128)
    om, oq, ov = reduce_weights(gm, gq, jnp.pad(sv, ((0, 4), (0, 0))))
    ov = ov.reshape(-1)
    return (
        lg.reshape(latent.shape),
        ov[0:D],
        oq[:, 0 : 3 * DA].reshape(4, 3, DA),
        oq[:, 3 * DA :].T,
        ov[5 * D : 5 * D + HEADS * 768].reshape(HEADS, 768)[:, :NREL],
        ov[D : 5 * D],
        om,
    )


def solution(mesh):
    placed = (
        P(None, "lat", "lon", None),
        P(),
        P(),
        P(None, None, "tp"),
        P("tp", None),
        P("tp", None),
        P(),
        P(None, "tp"),
        P(None, "lat", "lon", "tp"),
    )
    return jax.shard_map(
        local,
        mesh=mesh,
        in_specs=placed,
        out_specs=(
            P(None, "lat", "lon", None),
            P(),
            P(("lon", "lat"), None, "tp"),
            P("tp", ("lon", "lat")),
            P("tp", None),
            P(),
            P(("lon", "lat"), "tp"),
        ),
        check_vma=False,
    )
```

time: 1960 us -> 189 us (0.10)
  waiting for transfers between devices: 1100 us -> 0.01 us
  blocking collectives: 550 us -> 0 us
  Pallas kernels: 0 us -> 172 us
  other arithmetic: 133 us -> 0.74 us
  local copies, waits for them, and re-layouts: 112 us -> 12.1 us
  matrix products: 24.1 us -> 0 us
    reduce_scatter x1 -> x0, waiting for transfers between devices: 565 us -> none  [local(): lax.psum_scatter(lax.dot_general(columns, coarse_flat, (((0,), (0,)), (()...]
    psum x1 -> x0, blocking collectives: 550 us -> none  [local(): lax.psum((attn_gain_part, merge_gain_part, bias_part), ('lon', 'lat'))]
    unnamed x5 -> x0, waiting for transfers between devices: 416 us -> none
    pallas_call x0 -> x9, Pallas kernels: none -> 172 us  [call(): pl.pallas_call(kernel, out_shape=[jax.ShapeDtypeStruct(s, d) for s, d in...]
    scatter-add x1 -> x0, other arithmetic: 113 us -> none  [local(): jax.ops.segment_sum(score_total.T, rel.reshape(-1), rel_bias.shape[1])]
    psum x2 -> x0, waiting for transfers between devices: 88.2 us -> none  [the longest x1 59.7 us: local(): lax.psum(d_partial.astype(jnp.bfloat16), 'tp').astype(jnp.float32)]
    gather x2 -> x0, local copies, waits for them, and re-layouts: 47.1 us -> none  [local(): bias_block = jnp.take(rel_bias, rel, axis=1)]
    ppermute x8 -> x1, waiting for transfers between devices: 28.1 us -> 0.01 us  [local(): dmp = lax.ppermute(dmo, 'tp', [(0, 1), (1, 0)])]
  transfers between devices with their start and end apart: 12 -> 1, of which waited for: 10 -> 0; matrix products, arithmetic and copies ran while one was open for 10% -> 1% of each run, Pallas kernels for 0% -> 19%
where the time goes in v1:
time: 189 us; the launch traced here: 188 us
  Pallas kernels  172 us (91%)
  local copies, waits for them, and re-layouts  12.1 us (6%)
  starting transfers between devices  2.13 us (1%)
    pallas_call x9, Pallas kernels, call(): pl.pallas_call(kernel, out_shape=[jax.ShapeDtypeStruct(s, d) for s, d in...  172 us
  transfers between devices with their start and end apart: 1, of which 0 were waited for; matrix products, arithmetic and copies ran while one was open for 1% of the time, Pallas kernels for 19%

profile of v1, /device:TPU:2, one launch (start us, length us, event | category | flops | bytes accessed | tf_op | source)
XLA Modules:
  0.0 187.7 jit_solution(4981552704257733852)
XLA Ops:
  0.6 19.3 %way_in.1 = (bf16[768,512]{1,0:T(8,128)(2,1)}, bf16[224,512]{1,0:T(8,128)(2,1)}) custom-call(bf16[576,512]{1,0:T(8,128)(2,1)} %bitcast.29, bf16[144,512]{1,0:T(8,128)(2,1)} %bitcast.31, bf16[768,576]{1,0:T(8,128)(2,1)} %constant.23.clone.ql_ref, bf16[224,144]{1,0:T(8,128)(2,1)} %constant.30.clone.qc_ref), custom_call_target="tpu_custom_call" | custom-call | flops 1000000000 | bytes 8388608 | tf_op jit(solution)/shard_map/way_in/pallas_call | solution.py:164
  20.0 0.0 copy-start
  20.0 3.7 %coarse_cotangent.1 = (bf16[192,512]{1,0:T(8,128)(2,1)}, bf16[192,2048]{1,0:T(8,128)(2,1)}) custom-call(bf16[224,512]{1,0:T(8,128)(2,1)} %get-tuple-element.36.cc_ref, bf16[192,224]{1,0:T(8,128)(2,1)} %constant.31.clone.pc_ref, bf16[2048,512]{1,0:T(8,128)(2,1)} %mw_ref.1), custom_call_target="tpu_custom_call" | custom-call | flops 1000000000 | bytes 8388608 | tf_op jit(solution)/shard_map/coarse_cotangent/pallas_call | solution.py:164
  23.6 0.0 copy-start.2
  23.6 2.1 %collective-permute-start = (bf16[192,2048]{1,0:T(8,128)(2,1)}, bf16[192,2048]{1,0:T(8,128)(2,1)S(1)}, u32[]{:S(2)}, u32[]{:S(2)}) collective-permute-start(bf16[192,2048]{1,0:T(8,128)(2,1)} %get-tuple-element.37.dmo_ref), channel_id=1, source_target_pairs={{0,1},{1,0},{2,3},{3,2},{4,5},{5,4},{6,7},{7,6},{8,9},{9,8},{10,11... | collective-permute-start | bytes 2359304 | tf_op jit(solution)/shard_map/ppermute | solution.py:603
  25.8 0.0 copy-done
  25.8 0.3 copy.28
  26.1 1.2 copy.29.w_ref
  27.2 0.0 copy-done.2
  27.2 0.6 pad.8.tab_ref
  27.8 9.5 %attention_forward.1 = (bf16[576,512]{1,0:T(8,128)(2,1)}, bf16[576,768]{1,0:T(8,128)(2,1)}, f32[4,576,144]{2,1,0:T(8,128)}, bf16[576,512]{1,0:T(8,128)(2,1)}, bf16[576,256]{1,0:T(8,128)(2,1)}) custom-call(s32[48]{0:T(128)} %pole_ref.1, bf16[768,512]{1,0:T(8,128)(2,1)} %get-tuple-element.32.pc_ref, f32[1,512]{1,0:T(1,128)} %bitcast.32, ...), custom_call_target="tpu_custom_call" | custom-call | flops 4000000000 | bytes 8388608 | tf_op jit(solution)/shard_map/attention_forward/pallas_call | solution.py:164
  37.4 26.0 %attention_sums.1 = (bf16[576,512]{1,0:T(8,128)(2,1)}, bf16[4,96,512]{2,1,0:T(8,128)(2,1)}) custom-call(bf16[576,512]{1,0:T(8,128)(2,1)} %get-tuple-element.33.z_ref), custom_call_target="tpu_custom_call" | custom-call | flops 1000000000 | bytes 8388608 | tf_op jit(solution)/shard_map/attention_sums/pallas_call | solution.py:164
  63.4 0.0 collective-permute-done.dmp_ref
  63.4 0.0 copy-start.1
  63.5 0.9 copy-done.1
  64.3 6.8 %patch_merge.1 = (bf16[576,512]{1,0:T(8,128)(2,1)}, f32[2048,512]{1,0:T(8,128)}, f32[1,2048]{1,0:T(1,128)}) custom-call(bf16[768,512]{1,0:T(8,128)(2,1)} %get-tuple-element.32.pc_ref, bf16[768,768]{1,0:T(8,128)(2,1)} %constant.24.clone.pxm_ref, bf16[576,512]{1,0:T(8,128)(2,1)} %get-tuple-element.33.z_ref, bf16[576,512]{1,0:T(8,128)(2,1)} %get-tuple-element.34.zp_ref, ...), custom_call_target="tpu_custom_call" | custom-call | flops 1000000000 | bytes 8388608 | tf_op jit(solution)/shard_map/patch_merge/pallas_call | solution.py:164
  71.1 11.7 %attention_backward.1 = (bf16[608,512]{1,0:T(8,128)(2,1)}, bf16[608,512]{1,0:T(8,128)(2,1)}, f32[512,1024]{1,0:T(8,128)}, f32[4,768]{1,0:T(4,128)}) custom-call(bf16[576,512]{1,0:T(8,128)(2,1)} %get-tuple-element.39.dy_ref, bf16[576,576]{1,0:T(8,128)(2,1)} %constant.27.clone.pmw_ref, bf16[256,512]{1,0:T(8,128)(2,1)} %proj_ref.3, ...), custom_call_target="tpu_custom_call" | custom-call | flops 1000000000 | bytes 8388608 | tf_op jit(solution)/shard_map/attention_backward/pallas_call | solution.py:164
  82.9 0.7 copy.31
  83.6 32.4 %way_out.1 = (bf16[2,608,512]{2,1,0:T(8,128)(2,1)}, bf16[608,512]{1,0:T(8,128)(2,1)}) custom-call(bf16[608,512]{1,0:T(8,128)(2,1)} %get-tuple-element.44.dh_ref, bf16[608,512]{1,0:T(8,128)(2,1)} %get-tuple-element.45.dy_ref), custom_call_target="tpu_custom_call" | custom-call | flops 1000000000 | bytes 8388608 | tf_op jit(solution)/shard_map/way_out/pallas_call | solution.py:164
  116.0 0.0 copy-start.3
  116.0 4.5 %latent_cotangent.1 = (bf16[576,512]{1,0:T(8,128)(2,1)}, f32[1,512]{1,0:T(1,128)}) custom-call(bf16[576,512]{1,0:T(8,128)(2,1)} %bitcast.30, f32[1,512]{1,0:T(1,128)} %bitcast.33, bf16[576,608]{1,0:T(8,128)(2,1)} %constant.29.clone.pf_ref, bf16[2,608,512]{2,1,0:T(8,128)(2,1)} %get-tuple-element.46.dhr_ref, bf16[608,512]{1,0:T(8,128)(2,1)} %get-tuple-element.47.dyr_ref), custom_call_target="tpu_custom_call" | custom-call | flops 1000000000 | bytes 8388608 | tf_op jit(solution)/shard_map/latent_cotangent/pallas_call | solution.py:164
  120.5 0.0 copy-done.3
  120.5 0.7 maximum_reduce_fusion
  121.2 0.6 pad.9.sv_ref
  121.8 57.9 %weight_sums.1 = (f32[16,512]{1,0:T(8,128)}, f32[4,1024]{1,0:T(4,128)}, f32[48,128]{1,0:T(8,128)}) custom-call(f32[8,2,4,32,512]{4,3,2,1,0:T(8,128)} %bitcast.20, f32[8,2,4,8,1024]{4,3,2,1,0:T(8,128)} %bitcast.22, f32[48,128]{1,0:T(8,128)} %pad.9.sv_ref), custom_call_target="tpu_custom_call" | custom-call | flops 1000000000 | bytes 8388608 | tf_op jit(solution)/shard_map/weight_sums/pallas_call | solution.py:164
  179.8 1.3 slice_bitcast_fusion.1
  181.1 1.3 slice.27
  182.4 1.3 slice_bitcast_fusion.2
  183.6 1.3 slice_bitcast_fusion
  184.9 0.7 slice.29
  185.7 0.6 reshape.66
  186.3 1.4 copy.33
Async XLA Ops:
  20.0 5.8 %copy-start = (bf16[512,3,256]{2,0,1:T(8,128)(2,1)S(1)}, bf16[512,3,256]{2,0,1:T(8,128)(2,1)}, u32[]{:S(2)}) copy-start(bf16[512,3,256]{2,0,1:T(8,128)(2,1)} %param.22) | copy-start | bytes 2359300
  23.6 3.6 %copy-start.2 = (f32[4,759]{1,0:T(4,128)S(1)}, f32[4,759]{1,0:T(4,128)}, u32[]{:S(2)}) copy-start(f32[4,759]{1,0:T(4,128)} %param.24) | copy-start | bytes 36436
  23.6 39.8 %collective-permute-start = (bf16[192,2048]{1,0:T(8,128)(2,1)}, bf16[192,2048]{1,0:T(8,128)(2,1)S(1)}, u32[]{:S(2)}, u32[]{:S(2)}) collective-permute-start(bf16[192,2048]{1,0:T(8,128)(2,1)} %get-tuple-element.37.dmo_ref), channel_id=1, source_target_pairs={{0,1},{1,0},{2,3},{3,2},{4,5},{5,4},{6,7},{7,6},{8,9},{9,8},{10,11... | collective-permute-start | bytes 2359304 | tf_op jit(solution)/shard_map/ppermute | solution.py:603
  63.4 0.9 copy-start.1
  116.0 4.5 %copy-start.3 = (f32[1,2048]{1,0:T(1,128)S(1)}, f32[1,2048]{1,0:T(1,128)}, u32[]{:S(2)}) copy-start(f32[1,2048]{1,0:T(1,128)} %get-tuple-element.52) | copy-start | bytes 24580

commit v2 on v1

v2 whole, which is shorter than its diff:
```python
import functools

import jax
import jax.numpy as jnp
import numpy as np
from jax import lax
from jax.experimental import pallas as pl
from jax.experimental.pallas import tpu as pltpu
from jax.sharding import PartitionSpec as P

EPS = 1e-05
NEG = -1e30
MESH = pl.DeviceIdType.MESH
BF = jnp.bfloat16
F32 = jnp.float32

LEV, ROWS, COLS, D = 2, 6, 48, 512
WLON = 12
NWIN = COLS // WLON
WTOK = LEV * ROWS * WLON
TOK = LEV * ROWS * COLS
HEADS = 4
HD = 64
DA = HEADS * HD
NREL = 759
NZ, NY = 8, 4


(QL, QL2, QC, QC2, PC, PXM, PXW, PWM, PMW, PPO, PF, E0) = range(12)
MAPW = 768
IN_PADS = (336, 48, 336, 48)
OUT_PADS = (256, 48, 256, 48)
COARSE_PADS = (96, 16, 96, 16)


def pieces(row_sets, near, far, pads):
    base, out = 0, []
    parts = ((row_sets[0], near), (row_sets[0], far), (row_sets[1], near), (row_sets[1], far))
    for n, ((rows, cols), pad) in enumerate(zip(parts, pads)):
        p = base
        for l in range(LEV):
            for r in rows:
                for c in cols:
                    out.append((p, n, l, r, c))
                    p += 1
        base += pad
    return out


@functools.lru_cache(None)
def index_maps():
    t = np.full((24, MAPW), -1, np.int32)
    near, far = range(0, 42), range(42, 48)

    def merge_at(l, rr, sc):
        return ((rr * 2 + sc % 2) * LEV + l) * 24 + sc // 2

    def window_at(l, rr, sc):
        return (sc // WLON) * WTOK + (l * ROWS + rr - 1) * WLON + sc % WLON

    def seen(n, r, c):
        return (r + 4 if n < 2 else r - 2), (c + 6 if n % 2 == 0 else c - 42)

    for p, n, l, r, c in pieces((range(0, 4), range(2, 6)), near, far, IN_PADS):
        t[QL if n < 2 else QL2, (l * ROWS + r) * COLS + c] = p
        rr, sc = seen(n, r, c)
        t[PXM, p] = merge_at(l, rr, sc)
        if 1 <= rr <= 6:
            t[PXW, p] = window_at(l, rr, sc)
    for l in range(LEV):
        for rr in range(1, 7):
            for sc in range(COLS):
                t[PWM, window_at(l, rr, sc)] = merge_at(l, rr, sc) - 96
                t[PMW, merge_at(l, rr, sc) - 96] = window_at(l, rr, sc)
    for p, n, l, r, c in pieces((range(0, 3), range(3, 6)), near, far, OUT_PADS):
        rr, sc = seen(n, r, c)
        t[PPO, window_at(l, rr, sc)] = p
        t[PF, p] = (l * ROWS + r) * COLS + c
    for p, n, l, r, c in pieces((range(0, 2), range(1, 3)), range(0, 21), range(21, 24), COARSE_PADS):
        t[QC if n < 2 else QC2, (l * 3 + r) * 24 + c] = p
        cr = r + 2 if n < 2 else r - 1
        cc = c + 3 if n % 2 == 0 else c - 21
        t[PC, p] = (cr * LEV + l) * 24 + cc
    for c in range(WLON):
        for j in range(WTOK):
            l2, r2, c2 = j // 72, j // 12 % 6, j % 12
            t[E0 + c, ((1 - l2) * 11 + 5 - r2) * 23 + c - c2 + 11] = j
    return t


def pick(maps, n, rows, cols, base=0):
    at = lax.broadcasted_iota(jnp.int32, (rows, cols), 0) + base
    return jnp.where(at == maps[n : n + 1, 0:cols], 1.0, 0.0).astype(BF)


def mm(a, b):
    return lax.dot_general(a, b, (((1,), (0,)), ((), ())), preferred_element_type=F32)


def mm_nt(a, b):
    return lax.dot_general(a, b, (((1,), (1,)), ((), ())), preferred_element_type=F32)


def mm_tn(a, b):
    return lax.dot_general(a, b, (((0,), (0,)), ((), ())), preferred_element_type=F32)


def layer_stats(x):
    center = x - jnp.mean(x, -1, keepdims=True)
    inverse = lax.rsqrt(jnp.mean(center * center, -1, keepdims=True) + EPS)
    return center * inverse, inverse


def norm_back(up, gain, normed, inverse):
    s = up * gain
    return inverse * (
        s - jnp.mean(s, -1, keepdims=True) - normed * jnp.mean(s * normed, -1, keepdims=True)
    )


def head_mask(h, rows):
    lane = lax.broadcasted_iota(jnp.int32, (rows, DA), 1)
    return (lane >= h * HD) & (lane < (h + 1) * HD)


def stack_heads(x):
    zero = jnp.zeros_like(x)
    return jnp.concatenate(
        [jnp.where(head_mask(h, x.shape[0]), x, zero) for h in range(HEADS)], 0
    )


def vspec():
    return pl.BlockSpec(memory_space=pltpu.VMEM)


def call(kernel, name, ins, outs, scratch=(), cid=None, smem=0, flops=10**9, mib=16):
    params = dict(vmem_limit_bytes=mib << 20)
    if cid is not None:
        params.update(collective_id=cid, has_side_effects=True)
    specs = [pl.BlockSpec(memory_space=pltpu.SMEM)] * smem + [vspec()] * (len(ins) - smem)
    return pl.pallas_call(
        kernel,
        out_shape=[jax.ShapeDtypeStruct(s, d) for s, d in outs],
        in_specs=specs,
        out_specs=[vspec()] * len(outs),
        scratch_shapes=list(scratch),
        compiler_params=pltpu.CompilerParams(**params),
        cost_estimate=pl.CostEstimate(flops=flops, bytes_accessed=8 << 20, transcendentals=0),
        name=name,
    )(*ins)


def device(dlon, dlat, dtp):
    nlon, nlat = lax.axis_size("lon"), lax.axis_size("lat")
    return (
        lax.rem(lax.axis_index("lon") + dlon + nlon, nlon),
        lax.rem(lax.axis_index("lat") + dlat + nlat, nlat),
        lax.rem(lax.axis_index("tp") + dtp, 2),
    )


def greet(partners):
    barrier = pltpu.get_barrier_semaphore()
    for d in partners:
        pl.semaphore_signal(barrier, inc=1, device_id=d, device_id_type=MESH)
    pl.semaphore_wait(barrier, len(partners))


def remote(src, dst, ss, rs, n, dev):
    return pltpu.make_async_remote_copy(
        src, dst, ss.at[n], rs.at[n], device_id=dev, device_id_type=MESH
    )


def kin(
    maps, lat_ref, cg_ref, w_ref, proj_ref, tab_ref,
    pc_ref, cc_ref, wf, pf, tabs, sp, sc, ss, rs, ws, wr,
):
    tp, yy = lax.axis_index("tp"), lax.div(lax.axis_index("lat"), 2)
    peer = device(0, 0, 1)
    y_devs = [device(0, 2 * k, 0) for k in range(1, NY)]
    tabs[tp] = jnp.zeros((8, 768), F32)
    tabs[tp, 0:HEADS, 0:NREL] = tab_ref[...]
    greet(
        [peer]
        + y_devs
        + [device(s * o, s * a, 0) for s in (1, -1) for o, a in ((1, 0), (0, 1), (1, 1))]
    )
    at = pl.ds(pl.multiple_of(yy * 128, 128), 128)
    pat = pl.ds(pl.multiple_of(yy * 64, 64), 64)
    first = [
        remote(w_ref.at[:, at], wf.at[tp, :, at], ws, wr, 0, peer),
        remote(proj_ref.at[pat], pf.at[tp, pat], ws, wr, 1, peer),
        remote(tabs.at[tp], tabs.at[tp], ws, wr, 2, peer),
    ]
    for c in first:
        c.start()
    copies = []

    def send(n, m, k, lo, hi, clo, chi, dev):
        sp[lo:hi, :] = mm(pick(maps, m, hi - lo, TOK, lo), lat_ref[...]).astype(BF)
        c = remote(sp.at[lo:hi], pc_ref.at[lo:hi], ss, rs, 2 * n, dev)
        c.start()
        sc[clo:chi, :] = mm(pick(maps, k, chi - clo, 144, clo), cg_ref[...]).astype(BF)
        d = remote(sc.at[clo:chi], cc_ref.at[clo:chi], ss, rs, 2 * n + 1, dev)
        d.start()
        copies.extend([c, d])

    send(0, QL2, QC2, 384, 720, 112, 208, device(0, 1, 0))
    send(1, QL2, QC2, 720, 768, 208, 224, device(1, 1, 0))
    send(2, QL, QC, 336, 384, 96, 112, device(1, 0, 0))
    first[0].wait()
    first[1].wait()
    for k in range(1, NY):
        for n, ref in ((0, wf.at[1 - tp, :, at]), (1, pf.at[1 - tp, pat])):
            c = remote(ref, ref, ws, wr, 3 + 2 * (k - 1) + n, y_devs[k - 1])
            c.start()
            copies.append(c)
    pc_ref[0:336, :] = mm(pick(maps, QL, 336, TOK), lat_ref[...]).astype(BF)
    cc_ref[0:96, :] = mm(pick(maps, QC, 96, 144), cg_ref[...]).astype(BF)
    for n in range(3):
        wf[tp, n] = w_ref[n]
    pf[tp] = proj_ref[...]
    first[2].wait()
    for c in copies:
        c.wait()


def kdm(maps, cc_ref, mw_ref, cm_ref, dm_ref):
    cm_ref[...] = mm(pick(maps, PC, 192, 224), cc_ref[...]).astype(BF)
    for n in range(4):
        cols = slice(n * 512, (n + 1) * 512)
        dm_ref[:, cols] = mm_nt(cm_ref[...], mw_ref[cols, :]).astype(BF)


def kfwd(
    pole_ref, maps, pc_ref, gain_ref, wf, pf, tabs,
    y_ref, qkv_ref, p_ref, hn_ref, ao_ref, xw_ref, bm, u, wide,
):
    band = lax.axis_index("lat")
    nrows = pole_ref.shape[0]
    i = lax.broadcasted_iota(jnp.int32, (WTOK, WTOK), 0)
    j = lax.broadcasted_iota(jnp.int32, (WTOK, WTOK), 1)
    ri, rj = lax.rem(lax.div(i, WLON), ROWS), lax.rem(lax.div(j, WLON), ROWS)
    valid = jnp.zeros((WTOK, WTOK), jnp.int32)
    for r in range(ROWS):
        flag = pole_ref[lax.rem(band * ROWS + (r - 3 + nrows), nrows)]
        valid = jnp.where(rj == r, flag, valid)
    cut = jnp.where(band == 0, 3, 0)
    same = jnp.where(ri < cut, 1, 0) == jnp.where(rj < cut, 1, 0)
    allowed = (valid > 0) & same

    for g in range(2):
        for l in range(LEV):
            for r in range(ROWS):
                shift = (l * 11 + r) * 23
                row = tabs[g]
                if shift:
                    row = pltpu.roll(row, 768 - shift, 1)
                for h in range(HEADS):
                    n = (g * HEADS + h) * 12 + l * ROWS + r
                    u[n : n + 1, :] = row[h : h + 1, :512]
    t0 = u[...]
    hi = t0.astype(BF)
    rest = t0 - hi.astype(F32)
    mid = rest.astype(BF)
    low = (rest - mid.astype(F32)).astype(BF)
    split = jnp.concatenate([hi, mid, low], 0)
    for c in range(WLON):
        y = mm_nt(split, pick(maps, E0 + c, WTOK, 512))
        y = y[0:96] + y[96:192] + y[192:288]
        wide[0, pl.ds(c, 96, stride=WLON), :] = y[:, 0:128]
        wide[1, pl.ds(c, 96, stride=WLON), :] = jnp.concatenate(
            [y[:, 128:WTOK], jnp.zeros((96, 256 - WTOK), F32)], 1
        )
    for h in range(2 * HEADS):
        rows = slice(h * WTOK, (h + 1) * WTOK)
        both = jnp.concatenate([wide[0, rows, :], wide[1, rows, 0 : WTOK - 128]], 1)
        bm[h // HEADS, (h % HEADS) * WTOK : (h % HEADS + 1) * WTOK, :] = jnp.where(
            allowed, both, NEG
        )

    x = mm(pick(maps, PXW, TOK, 768), pc_ref[...])
    xw_ref[...] = x.astype(BF)
    normed, _ = layer_stats(x)
    hn_ref[...] = (normed * gain_ref[...]).astype(BF)
    for g in range(2):
        for n in range(3):
            qkv_ref[g, :, n * DA : (n + 1) * DA] = mm(hn_ref[...], wf[g, n]).astype(BF)

    def window(n, carry):
        g, w = lax.div(n, NWIN), lax.rem(n, NWIN)
        rows = pl.ds(pl.multiple_of(w * WTOK, 16), WTOK)
        q = qkv_ref[g, rows, 0:DA]
        k = qkv_ref[g, rows, DA : 2 * DA]
        v = qkv_ref[g, rows, 2 * DA : 3 * DA]
        s = mm_nt(stack_heads(q), k) * (HD**-0.5) + bm[g]
        e = jnp.exp(s - jnp.max(s, -1, keepdims=True))
        p = e / jnp.sum(e, -1, keepdims=True)
        p_ref[g, w] = p
        pb = p.astype(BF)
        vs = stack_heads(v)
        o = jnp.zeros((WTOK, DA), F32)
        for h in range(HEADS):
            at = slice(h * WTOK, (h + 1) * WTOK)
            o = o + mm(pb[at], vs[at])
        ao_ref[g, rows, :] = o.astype(BF)
        return carry

    lax.fori_loop(0, 2 * NWIN, window, 0)
    to_merge = pick(maps, PWM, TOK, TOK)
    y = mm(pick(maps, PXM, TOK, 768, 96), pc_ref[...])
    for g in range(2):
        y = y + mm(mm(to_merge, ao_ref[g]).astype(BF), pf[g])
    y_ref[...] = y.astype(BF)


def kmerge(
    y_ref, dmo_ref, dmp_ref, cm_ref, gain_ref, dy_ref, gm_ref, mg_ref, yh, mb, ss, rs
):
    nxt, prev = device(0, 1, 0), device(0, -1, 0)
    greet([nxt, prev])
    copies = [
        remote(y_ref.at[480:576], yh.at[0], ss, rs, 0, nxt),
        remote(y_ref.at[0:96], yh.at[1], ss, rs, 1, prev),
    ]
    for c in copies:
        c.start()
    gain = gain_ref[...]
    acc = jnp.zeros((1, 4 * D), F32)

    def slab(r, cp):
        lo = cp * 48
        if r == 0:
            return yh[0, lo : lo + 48, :]
        if r == 7:
            return yh[1, lo : lo + 48, :]
        lo += (r - 1) * 96
        return y_ref[lo : lo + 48, :]

    for cr in (1, 2, 0, 3):
        if cr == 0:
            for c in copies:
                c.wait()
        slabs = [slab(2 * cr + rp, cp) for rp in (0, 1) for cp in (0, 1)]
        hat, inv = layer_stats(jnp.concatenate(slabs, 1).astype(F32))
        at = slice(cr * 48, (cr + 1) * 48)
        dm = dmo_ref[at, :].astype(F32) + dmp_ref[at, :].astype(F32)
        if cr > 0:
            acc = acc + jnp.sum(dm * hat, 0, keepdims=True)
            mb[(cr - 1) * 48 : cr * 48, :] = (hat * gain).astype(BF)
        dy = norm_back(dm, gain, hat, inv).astype(BF)
        for q in range(4):
            r = 2 * cr + q // 2
            if 1 <= r <= 6:
                lo = (r - 1) * 96 + (q % 2) * 48
                dy_ref[lo : lo + 48, :] = dy[:, q * D : (q + 1) * D]
    mg_ref[...] = acc
    for n in range(4):
        at = slice(n * 512, (n + 1) * 512)
        gm_ref[at, :] = mm_tn(mb[:, at], cm_ref[48:192, :])


def ktail(
    maps, dy_ref, gain_ref, wf, pf, qkv_ref, p_ref, hn_ref, ao_ref, xw_ref, gm_ref, mg_ref,
    rp_ref, om_ref, oq_ref, ov_ref,
    dyw, do, dqkv, dst, t, wide, gq, lp, sv,
    sm1, sq1, rm1, rq1, sv1,
    am, aq, sm2, sq2, rm2, rq2, sv2,
    bmm, bq, sm3, rm3, rq3, sv3,
    cm, cq, rm4, rq4, sv4, ss, rs,
):
    lon, lat, tp = lax.axis_index("lon"), lax.axis_index("lat"), lax.axis_index("tp")
    z, core = lax.div(lon, 2), lax.rem(lon, 2)
    yy, xx = lax.div(lat, 2), lax.rem(lat, 2)
    core_dev = (z * 2 + 1 - core, lat, tp)
    x_dev = (lon, yy * 2 + 1 - xx, tp)
    y_devs = [(lon, lax.rem(yy + k, NY) * 2 + xx, tp) for k in range(1, NY)]
    z_devs = [(lax.rem(z + k, NZ) * 2 + core, lat, tp) for k in range(1, NZ)]
    outward = ((-1, 0), (0, -1), (-1, -1))
    greet(
        [core_dev, x_dev]
        + y_devs
        + z_devs
        + [device(s * o, s * a, 0) for s in (1, -1) for o, a in outward]
    )
    scale = HD**-0.5

    def start(copies):
        for c in copies:
            c.start()
        return copies

    def wait(copies):
        for c in copies:
            c.wait()

    for iy in range(NY):
        for iz in range(NZ):
            sm1[iy, iz] = gm_ref[iz, 1 - core, iy].astype(BF)
    m1 = start([remote(sm1, rm1, ss, rs, 0, core_dev)])

    dyw[...] = mm(pick(maps, PMW, TOK, TOK), dy_ref[...]).astype(BF)
    for g in range(2):
        do[g] = mm_nt(dyw[...], pf[g]).astype(BF)
    dst[...] = jnp.zeros_like(dst)

    def window(n, carry):
        g, w = lax.div(n, NWIN), lax.rem(n, NWIN)
        rows = pl.ds(pl.multiple_of(w * WTOK, 16), WTOK)
        q = qkv_ref[g, rows, 0:DA]
        k = qkv_ref[g, rows, DA : 2 * DA]
        v = qkv_ref[g, rows, 2 * DA : 3 * DA]
        p = p_ref[g, w]
        dos = stack_heads(do[g, rows, :])
        dp = mm_nt(dos, v)
        dv = mm_tn(p.astype(BF), dos)
        ds = p * (dp - jnp.sum(dp * p, -1, keepdims=True))
        dst[g] = dst[g] + ds
        dsb = ds.astype(BF)
        dk = mm_tn(dsb, stack_heads(q)) * scale
        ks = stack_heads(k)
        dq = jnp.zeros((WTOK, DA), F32)
        for h in range(HEADS):
            at = slice(h * WTOK, (h + 1) * WTOK)
            dq = dq + mm(dsb[at], ks[at])
        dqkv[g, 0, rows, :] = (dq * scale).astype(BF)
        dqkv[g, 1, rows, :] = dk.astype(BF)
        dqkv[g, 2, rows, :] = dv.astype(BF)
        return carry

    lax.fori_loop(0, NWIN, window, 0)

    wait(m1)
    m2 = []
    for k in range(1, NY):
        iy = lax.rem(yy + k, NY)
        for iz in range(NZ):
            sm2[k - 1, iz] = (gm_ref[iz, core, iy] + rm1[iy, iz].astype(F32)).astype(BF)
        m2 += start([remote(sm2.at[k - 1], rm2.at[k - 1], ss, rs, k, y_devs[k - 1])])
    for iz in range(NZ):
        am[iz] = gm_ref[iz, core, yy] + rm1[yy, iz].astype(F32)

    lax.fori_loop(NWIN, 2 * NWIN, window, 0)

    for n in range(3):
        part = mm_tn(hn_ref[...], dqkv[tp, n])
        for iz in range(NZ):
            for ic in range(2):
                for iy in range(NY):
                    lo = ((iz * 2 + ic) * NY + iy) * 8
                    gq[iz, ic, iy, :, n * DA : (n + 1) * DA] = part[lo : lo + 8, :]
    part = mm_tn(dyw[...], ao_ref[tp])
    for iz in range(NZ):
        for ic in range(2):
            for iy in range(NY):
                lo = ((iz * 2 + ic) * NY + iy) * 8
                gq[iz, ic, iy, :, 3 * DA :] = part[lo : lo + 8, :]
    for iy in range(NY):
        for iz in range(0, NZ, 2):
            pair = jnp.concatenate([gq[iz, 1 - core, iy], gq[iz + 1, 1 - core, iy]], 0)
            sq1[iy, iz * 8 : iz * 8 + 16, :] = pair.astype(BF)
    q1 = start([remote(sq1, rq1, ss, rs, 12, core_dev)])

    dh = jnp.zeros((TOK, D), F32)
    for g in range(2):
        for n in range(3):
            dh = dh + mm_nt(dqkv[g, n], wf[g, n])
    normed, inv = layer_stats(xw_ref[...].astype(F32))
    ag = jnp.sum(dh * normed, 0, keepdims=True)
    branch = norm_back(dh, gain_ref[...], normed, inv).astype(BF)
    lg = (dyw[...].astype(F32) + branch.astype(F32)).astype(BF)
    lp[...] = mm(pick(maps, PPO, 608, TOK), lg).astype(BF)
    ro = []
    for n, (lo, hi) in enumerate(((256, 304), (304, 560), (560, 608))):
        dev = device(outward[n][0], outward[n][1], 0)
        ro += start([remote(lp.at[lo:hi], rp_ref.at[lo:hi], ss, rs, 13 + n, dev)])
    rp_ref[0:256, :] = lp[0:256, :]

    wide[0] = dst[tp, :, 0:128]
    wide[1, :, 0 : WTOK - 128] = dst[tp, :, 128:WTOK]
    acc = jnp.zeros((48, 512), F32)
    for c in range(WLON):
        rows = pl.ds(c, 48, stride=WLON)
        x = jnp.concatenate([wide[0, rows, :], wide[1, rows, :][:, 0 : WTOK - 128]], 1)
        hi = x.astype(BF)
        low = (x - hi.astype(F32)).astype(BF)
        y = mm(jnp.concatenate([hi, low], 0), pick(maps, E0 + c, WTOK, 512))
        acc = acc + y[0:48] + y[48:96]
    t[:, 0:512] = acc
    t[:, 512:768] = jnp.zeros((48, 256), F32)
    for h in range(HEADS):
        out = jnp.zeros((1, 768), F32)
        for g in range(12):
            row = t[h * 12 + g : h * 12 + g + 1, :]
            shift = (g // ROWS * 11 + g % ROWS) * 23
            out = out + (pltpu.roll(row, shift, 1) if shift else row)
        sv[h : h + 1, :] = out
    sv[4:5, :] = mg_ref[:, 0:768]
    sv[5:6, :] = mg_ref[:, 768:1536]
    sv[6:7, 0:512] = mg_ref[:, 1536:2048]
    sv[6:7, 512:768] = jnp.zeros((1, 256), F32)
    sv[7:8, 0:512] = ag
    sv[7:8, 512:768] = jnp.zeros((1, 256), F32)
    sv1[core] = sv[...]
    v1 = start([remote(sv1.at[core], sv1.at[core], ss, rs, 16, core_dev)])

    wait(m2)
    for iz in range(NZ):
        acc = am[iz]
        for k in range(NY - 1):
            acc = acc + rm2[k, iz].astype(F32)
        bmm[iz] = acc
    m3 = []
    for k in range(1, NZ):
        sm3[k - 1] = bmm[lax.rem(z + k, NZ)].astype(BF)
        m3 += start([remote(sm3.at[k - 1], rm3.at[k - 1], ss, rs, 16 + k, z_devs[k - 1])])

    wait(q1)
    q2 = []
    for k in range(1, NY):
        iy = lax.rem(yy + k, NY)
        for iz in range(0, NZ, 2):
            pair = jnp.concatenate([gq[iz, core, iy], gq[iz + 1, core, iy]], 0)
            at = slice(iz * 8, iz * 8 + 16)
            sq2[k - 1, at, :] = (pair + rq1[iy, at, :].astype(F32)).astype(BF)
        q2 += start([remote(sq2.at[k - 1], rq2.at[k - 1], ss, rs, 23 + k, y_devs[k - 1])])
    for iz in range(0, NZ, 2):
        pair = jnp.concatenate([gq[iz, core, yy], gq[iz + 1, core, yy]], 0)
        at = slice(iz * 8, iz * 8 + 16)
        aq[at, :] = pair + rq1[yy, at, :].astype(F32)
    wait(v1)
    sv2[yy] = sv1[0] + sv1[1]
    v2 = start(
        [
            remote(sv2.at[yy], sv2.at[yy], ss, rs, 26 + k, y_devs[k - 1])
            for k in range(1, NY)
        ]
    )

    wait(m3)
    acc = bmm[z]
    for k in range(NZ - 1):
        acc = acc + rm3[k].astype(F32)
    cm[0] = acc[0:16]
    cm[1] = acc[16:32]
    m4 = start([remote(cm.at[1 - xx], rm4, ss, rs, 30, x_dev)])

    wait(q2)
    acc = aq[...]
    for k in range(NY - 1):
        acc = acc + rq2[k].astype(F32)
    for iz in range(NZ):
        bq[iz] = acc[iz * 8 : iz * 8 + 8]
    q3 = start(
        [
            remote(bq.at[lax.rem(z + k, NZ)], rq3.at[k - 1], ss, rs, 30 + k, z_devs[k - 1])
            for k in range(1, NZ)
        ]
    )
    wait(v2)
    sv3[z] = sv2[0] + sv2[1] + sv2[2] + sv2[3]
    v3 = start(
        [
            remote(sv3.at[z], sv3.at[z], ss, rs, 37 + k, z_devs[k - 1])
            for k in range(1, NZ)
        ]
    )
    wait(q3)
    acc = bq[z]
    for k in range(NZ - 1):
        acc = acc + rq3[k]
    cq[...] = acc
    q4 = start([remote(cq, rq4, ss, rs, 45, x_dev)])
    wait(v3)
    acc = sv3[0]
    for k in range(1, NZ):
        acc = acc + sv3[k]
    sv4[xx] = acc
    v4 = start([remote(sv4.at[xx], sv4.at[xx], ss, rs, 46, x_dev)])
    wait(m4)
    om_ref[...] = cm[xx] + rm4[...]
    wait(q4)
    oq_ref[...] = cq[...] + rq4[...]
    wait(v4)
    ov_ref[...] = sv4[0] + sv4[1]
    wait(ro)


def kend(
    maps, rp_ref, om_ref, oq_ref, ov_ref, lg_ref, ag_ref, gw_ref, gp_ref, gb_ref, mg_ref, gm_ref
):
    xx = lax.rem(lax.axis_index("lat"), 2)
    lg_ref[...] = mm(pick(maps, PF, TOK, 608), rp_ref[...]).astype(BF)
    gm_ref[...] = om_ref[...]
    mine = jnp.where(xx == 0, oq_ref[0:4, :], oq_ref[4:8, :])
    for n in range(3):
        gw_ref[n] = mine[:, n * DA : (n + 1) * DA]
    gp_ref[...] = mine[:, 3 * DA :]
    gb_ref[...] = ov_ref[0:HEADS, 0:NREL]
    mg_ref[:, 0:768] = ov_ref[4:5, :]
    mg_ref[:, 768:1536] = ov_ref[5:6, :]
    mg_ref[:, 1536:2048] = ov_ref[6:7, 0:512]
    ag_ref[...] = ov_ref[7:8, 0:512]


def local(
    latent, pole_mask, attn_gain, qkv_weight, proj_weight, rel_bias, merge_gain, merge_weight,
    coarse_grad,
):
    maps = jnp.asarray(index_maps())
    dma = pltpu.SemaphoreType.DMA
    lat = latent.reshape(TOK, D)
    gain = attn_gain.reshape(1, D)
    vm = pltpu.VMEM

    pc, cc, wf, pf, tabs = call(
        kin, "way_in",
        [maps, lat, coarse_grad.reshape(144, 512), qkv_weight.transpose(1, 0, 2), proj_weight, rel_bias],
        [
            ((768, D), BF), ((224, 512), BF), ((2, 3, D, DA), BF), ((2, DA, D), BF),
            ((2, 8, 768), F32),
        ],
        [vm((768, D), BF), vm((224, 512), BF), dma((6,)), dma((6,)), dma((9,)), dma((9,))],
        cid=1, mib=16,
    )
    cm, dmo = call(
        kdm, "coarse_cotangent", [maps, cc, merge_weight],
        [((192, 512), BF), ((192, 4 * D), BF)], mib=10,
    )
    dmp = lax.ppermute(dmo, "tp", [(0, 1), (1, 0)])
    nb = HEADS * WTOK
    y, qkv, p, hn, ao, xw = call(
        kfwd, "attention_forward", [pole_mask, maps, pc, gain, wf, pf, tabs],
        [
            ((TOK, D), BF), ((2, TOK, 3 * DA), BF), ((2, NWIN, nb, WTOK), F32),
            ((TOK, D), BF), ((2, TOK, DA), BF), ((TOK, D), BF),
        ],
        [vm((2, nb, WTOK), F32), vm((96, 512), F32), vm((2, 2 * nb, 128), F32)],
        smem=1, flops=8 * 10**9, mib=28,
    )
    dy, gm, mg = call(
        kmerge, "patch_merge", [y, dmo, dmp, cm, merge_gain.reshape(1, 4 * D)],
        [((TOK, D), BF), ((4 * D, 512), F32), ((1, 4 * D), F32)],
        [vm((2, 96, D), BF), vm((144, 4 * D), BF), dma((2,)), dma((2,))],
        cid=2, mib=20,
    )
    nv = (8, 768)
    rp, om, oq, ov = call(
        ktail, "attention_backward",
        [maps, dy, gain, wf, pf, qkv, p, hn, ao, xw, gm.reshape(NZ, 2, NY, 32, 512), mg],
        [((608, D), BF), ((16, 512), F32), ((8, 1024), F32), (nv, F32)],
        [
            vm((TOK, D), BF), vm((2, TOK, DA), BF), vm((2, 3, TOK, DA), BF),
            vm((2, nb, WTOK), F32), vm((48, 768), F32), vm((2, nb, 128), F32),
            vm((NZ, 2, NY, 8, 1024), F32), vm((608, D), BF), vm(nv, F32),
            vm((NY, NZ, 32, 512), BF), vm((NY, 64, 1024), BF),
            vm((NY, NZ, 32, 512), BF), vm((NY, 64, 1024), BF), vm((2,) + nv, F32),
            vm((NZ, 32, 512), F32), vm((64, 1024), F32),
            vm((NY - 1, NZ, 32, 512), BF), vm((NY - 1, 64, 1024), BF),
            vm((NY - 1, NZ, 32, 512), BF), vm((NY - 1, 64, 1024), BF), vm((NY,) + nv, F32),
            vm((NZ, 32, 512), F32), vm((NZ, 8, 1024), F32),
            vm((NZ - 1, 32, 512), BF), vm((NZ - 1, 32, 512), BF),
            vm((NZ - 1, 8, 1024), F32), vm((NZ,) + nv, F32),
            vm((2, 16, 512), F32), vm((8, 1024), F32),
            vm((16, 512), F32), vm((8, 1024), F32), vm((2,) + nv, F32),
            dma((48,)), dma((48,)),
        ],
        cid=3, mib=44,
    )
    lg, ag, gw, gp, gb, mgg, gmm = call(
        kend, "finish", [maps, rp, om, oq, ov],
        [
            ((TOK, D), BF), ((1, D), F32), ((3, 4, DA), F32), ((4, DA), F32),
            ((HEADS, NREL), F32), ((1, 4 * D), F32), ((16, 512), F32),
        ],
        mib=8,
    )
    return (
        lg.reshape(latent.shape),
        ag.reshape(D),
        gw.transpose(1, 0, 2),
        gp.T,
        gb,
        mgg.reshape(4 * D),
        gmm,
    )


def solution(mesh):
    placed = (
        P(None, "lat", "lon", None),
        P(),
        P(),
        P(None, None, "tp"),
        P("tp", None),
        P("tp", None),
        P(),
        P(None, "tp"),
        P(None, "lat", "lon", "tp"),
    )
    return jax.shard_map(
        local,
        mesh=mesh,
        in_specs=placed,
        out_specs=(
            P(None, "lat", "lon", None),
            P(),
            P(("lon", "lat"), None, "tp"),
            P("tp", ("lon", "lat")),
            P("tp", None),
            P(),
            P(("lon", "lat"), "tp"),
        ),
        check_vma=False,
    )
```

time: 189 us -> 134 us (0.71)
  Pallas kernels: 172 us -> 118 us
  waiting for transfers between devices: 0.01 us -> 3.19 us
  local copies, waits for them, and re-layouts: 12.1 us -> 9.79 us
    pallas_call x9 -> x6, Pallas kernels: 172 us -> 118 us  [call(): pl.pallas_call(kernel, out_shape=[jax.ShapeDtypeStruct(s, d) for s, d in...]
    unnamed x11 -> x26, local copies, waits for them, and re-layouts: 3.28 us -> 9.79 us
    slice x4 -> x0, local copies, waits for them, and re-layouts: 4.59 us -> none  [the longest x1 1.31 us: local(): ov[D:5 * D]]
    ppermute x1, waiting for transfers between devices: 0.01 us -> 3.19 us  [local(): dmp = lax.ppermute(dmo, 'tp', [(0, 1), (1, 0)])]
  transfers between devices with their start and end apart: 1 -> 1, of which waited for: 0 -> 1; matrix products, arithmetic and copies ran while one was open for 1% -> 0% of each run, Pallas kernels for 19% -> 8%
where the time goes in v2:
time: 134 us; the launch traced here: 133 us
  Pallas kernels  118 us (88%)
  local copies, waits for them, and re-layouts  9.79 us (7%)
  waiting for transfers between devices  3.19 us (2%)
    pallas_call x6, Pallas kernels, call(): pl.pallas_call(kernel, out_shape=[jax.ShapeDtypeStruct(s, d) for s, d in...  118 us
    unnamed x26, local copies, waits for them, and re-layouts  9.79 us
    ppermute x1, waiting for transfers between devices, local(): dmp = lax.ppermute(dmo, 'tp', [(0, 1), (1, 0)])  3.19 us
  transfers between devices with their start and end apart: 1, of which 1 were waited for; matrix products, arithmetic and copies ran while one was open for 0% of the time, Pallas kernels for 8%

profile of v2, /device:TPU:2, one launch (start us, length us, event | category | flops | bytes accessed | tf_op | source)
XLA Modules:
  0.0 133.2 jit_solution(17437236103251505047)
XLA Ops:
  0.6 0.0 copy-start.2
  0.6 0.9 copy-done.2
  1.5 0.0 copy-start.6
  1.5 1.1 copy-done.6
  2.7 0.0 copy-start.7
  2.7 1.1 copy-done.7
  3.7 0.0 copy-start.8
  3.7 0.9 copy-done.8
  4.7 0.0 copy-start.9
  4.7 0.9 copy-done.9
  5.6 0.0 copy-start.10
  5.6 0.7 copy-done.10
  6.3 0.0 copy-start.5
  6.3 26.3 %way_in.1 = (bf16[768,512]{1,0:T(8,128)(2,1)S(1)}, bf16[224,512]{1,0:T(8,128)(2,1)S(1)}, bf16[2,3,512,256]{3,2,1,0:T(8,128)(2,1)S(1)}, bf16[2,256,512]{2,1,0:T(8,128)(2,1)S(1)}, f32[2,8,768]{2,1,0:T(8,128)S(1)}) custom-call(s32[24,768]{1,0:T(8,128)S(1)} %copy-done.2, bf16[576,512]{1,0:T(8,128)(2,1)S(1)} %bitcast.15, bf16[144,512]{1,0:T(8,128)(2,1)S(1)} %bitcast.16, ...), custom_call_target="tpu_custom_call" | custom-call | flops 1000000000 | bytes 8388608 | tf_op jit(solution)/shard_map/way_in/pallas_call | solution.py:142
  32.6 0.0 copy-start.3
  32.6 0.0 copy-start.4
  32.6 0.0 copy-start.12
  32.6 0.0 copy-done.5
  32.6 0.9 coarse_cotangent.1
  33.6 1.2 collective-permute-start
  34.8 0.0 copy-done.3
  34.8 0.0 copy-done.4
  34.8 0.0 copy-done.12
  34.8 0.0 copy-start.11
  34.8 11.2 %attention_forward.1 = (bf16[576,512]{1,0:T(8,128)(2,1)S(1)}, bf16[2,576,768]{2,1,0:T(8,128)(2,1)S(1)}, f32[2,4,576,144]{3,2,1,0:T(8,128)S(1)}, bf16[576,512]{1,...) custom-call(s32[48]{0:T(128)S(1)} %copy-done.12, s32[24,768]{1,0:T(8,128)S(1)} %copy-done.3, ...), custom_call_target="tpu_custom_call" | custom-call | flops 8000000000 | bytes 8388608 | tf_op jit(solution)/shard_map/attention_forward/pallas_call | solution.py:142
  46.0 0.0 copy-start
  46.0 2.1 %copy-done = f32[2,4,576,144]{3,2,1,0:T(8,128)} copy-done((f32[2,4,576,144]{3,2,1,0:T(8,128)}, f32[2,4,576,144]{3,2,1,0:T(8,128)S(1)}, u32[]{:S(2)}) %copy-start) | copy-done | bytes 2654232
  48.1 3.2 %collective-permute-done.dmp_ref = bf16[192,2048]{1,0:T(8,128)(2,1)S(1)} collective-permute-done((bf16[192,2048]{1,0:T(8,128)(2,1)S(1)}, bf16[192,2048]{1,0:T(8,128)(2,1)S(1)}, u32[]{:S(2)}, u32[]{:S(2)}) %collective-permute-start) | collective-permute-done | bytes 786464 | tf_op jit(solution)/shard_map/ppermute | solution.py:632
  51.3 0.0 copy-done.11
  51.3 15.9 %patch_merge.1 = (bf16[576,512]{1,0:T(8,128)(2,1)S(1)}, f32[2048,512]{1,0:T(8,128)S(1)}, f32[1,2048]{1,0:T(1,128)S(1)}) custom-call(bf16[576,512]{1,0:T(8,128)(2,1)S(1)} %get-tuple-element.38.y_ref, bf16[192,2048]{1,0:T(8,128)(2,1)S(1)} %get-tuple-element.40.dmo_ref, bf16[192,2048]{1,0:T(8,128)(2,1)S(1)} %collective-permute-done.dmp_ref, ...), custom_call_target="tpu_custom_call" | custom-call | flops 1000000000 | bytes 8388608 | tf_op jit(solution)/shard_map/patch_merge/pallas_call | solution.py:142
  67.2 0.0 copy-start.1
  67.2 2.0 %copy-done.1 = f32[2048,512]{1,0:T(8,128)} copy-done((f32[2048,512]{1,0:T(8,128)}, f32[2048,512]{1,0:T(8,128)S(1)}, u32[]{:S(2)}) %copy-start.1) | copy-done | bytes 4194328
  69.2 62.5 %attention_backward.1 = (bf16[608,512]{1,0:T(8,128)(2,1)S(1)}, f32[16,512]{1,0:T(8,128)S(1)}, f32[8,1024]{1,0:T(8,128)S(1)}, f32[8,768]{1,0:T(8,128)S(1)}) custom-call(s32[24,768]{1,0:T(8,128)S(1)} %copy-done.3, bf16[576,512]{1,0:T(8,128)(2,1)S(1)} %get-tuple-element.42.dy_ref, f32[1,512]{1,0:T(1,128)S(1)} %bitcast.13, ...), custom_call_target="tpu_custom_call" | custom-call | flops 1000000000 | bytes 8388608 | tf_op jit(solution)/shard_map/attention_backward/pallas_call | solution.py:142
  131.7 1.4 %finish.1 = (bf16[576,512]{1,0:T(8,128)(2,1)}, f32[1,512]{1,0:T(1,128)}, f32[3,4,256]{2,1,0:T(4,128)}, f32[4,256]{1,0:T(4,128)}, f32[4,759]{1,0:T(4,128)}, /*index=5*/f32[1,2048]{1,0:T(1,128)}, f32[16,512]{1,0:T(8,128)}) custom-call(s32[24,768]{1,0:T(8,128)S(1)} %copy-done.3, bf16[608,512]{1,0:T(8,128)(2,1)S(1)} %get-tuple-element.50.rp_ref, ...), custom_call_target="tpu_custom_call" | custom-call | flops 1000000000 | bytes 8388608 | tf_op jit(solution)/shard_map/finish/pallas_call | solution.py:142
Async XLA Ops:
  0.6 0.9 copy-start.2
  1.5 1.1 copy-start.6
  2.7 1.1 copy-start.7
  3.7 0.9 copy-start.8
  4.7 0.9 copy-start.9
  5.6 0.7 copy-start.10
  6.3 26.3 %copy-start.5 = (bf16[2048,512]{1,0:T(8,128)(2,1)S(1)}, bf16[2048,512]{1,0:T(8,128)(2,1)}, u32[]{:S(2)}) copy-start(bf16[2048,512]{1,0:T(8,128)(2,1)} %mw_ref.1) | copy-start | bytes 6291460
  32.6 2.2 %copy-start.3 = (s32[24,768]{1,0:T(8,128)S(1)}, s32[24,768]{1,0:T(8,128)}, u32[]{:S(2)}) copy-start(s32[24,768]{1,0:T(8,128)} %constant.2.clone.maps) | copy-start | bytes 221188
  32.6 2.2 %copy-start.4 = (f32[512]{0:T(512)S(1)}, f32[512]{0:T(512)}, u32[]{:S(2)}) copy-start(f32[512]{0:T(512)} %param.12) | copy-start | bytes 6148
  32.6 2.2 %copy-start.12 = (s32[48]{0:T(128)S(1)}, s32[48]{0:T(128)}, u32[]{:S(2)}) copy-start(s32[48]{0:T(128)} %pole_ref.1) | copy-start | bytes 580
  33.6 17.7 %collective-permute-start = (bf16[192,2048]{1,0:T(8,128)(2,1)S(1)}, bf16[192,2048]{1,0:T(8,128)(2,1)S(1)}, u32[]{:S(2)}, u32[]{:S(2)}) collective-permute-start(bf16[192,2048]{1,0:T(8,128)(2,1)S(1)} %get-tuple-element.40.dmo_ref), channel_id=1, source_target_pairs={{0,1},{1,0},{2,3},{3,2},{4,5},{5,4},{6,7},{7,6},{8,9},{9,8},{10,11... | collective-permute-start | bytes 2359304 | tf_op jit(solution)/shard_map/ppermute | solution.py:632
  34.8 16.5 %copy-start.11 = (f32[2048]{0:T(1024)S(1)}, f32[2048]{0:T(1024)}, u32[]{:S(2)}) copy-start(f32[2048]{0:T(1024)} %param.16) | copy-start | bytes 24580
  46.0 2.1 %copy-start = (f32[2,4,576,144]{3,2,1,0:T(8,128)}, f32[2,4,576,144]{3,2,1,0:T(8,128)S(1)}, u32[]{:S(2)}) copy-start(f32[2,4,576,144]{3,2,1,0:T(8,128)S(1)} %get-tuple-element.44.p_ref) | copy-start | bytes 7962628
  67.2 2.0 %copy-start.1 = (f32[2048,512]{1,0:T(8,128)}, f32[2048,512]{1,0:T(8,128)S(1)}, u32[]{:S(2)}) copy-start(f32[2048,512]{1,0:T(8,128)S(1)} %get-tuple-element.48) | copy-start | bytes 12582916

commit v3 on v2

v3 whole, which is shorter than its diff:
```python
import functools

import jax
import jax.numpy as jnp
import numpy as np
from jax import lax
from jax.experimental import pallas as pl
from jax.experimental.pallas import tpu as pltpu
from jax.sharding import PartitionSpec as P

EPS = 1e-05
NEG = -1e30
MESH = pl.DeviceIdType.MESH
BF = jnp.bfloat16
F32 = jnp.float32

LEV, ROWS, COLS, D = 2, 6, 48, 512
WLON = 12
NWIN = COLS // WLON
WTOK = LEV * ROWS * WLON
TOK = LEV * ROWS * COLS
HEADS = 4
HD = 64
DA = HEADS * HD
NREL = 759
NZ, NY = 8, 4


(QL, QL2, QC, QC2, PC, PXM, PXW, PWM, PMW, PPO, PF, E0) = range(12)
MAPW = 768
IN_PADS = (336, 48, 336, 48)
OUT_PADS = (256, 48, 256, 48)
COARSE_PADS = (96, 16, 96, 16)


def pieces(row_sets, near, far, pads):
    base, out = 0, []
    parts = ((row_sets[0], near), (row_sets[0], far), (row_sets[1], near), (row_sets[1], far))
    for n, ((rows, cols), pad) in enumerate(zip(parts, pads)):
        p = base
        for l in range(LEV):
            for r in rows:
                for c in cols:
                    out.append((p, n, l, r, c))
                    p += 1
        base += pad
    return out


@functools.lru_cache(None)
def index_maps():
    t = np.full((24, MAPW), -1, np.int32)
    near, far = range(0, 42), range(42, 48)

    def merge_at(l, rr, sc):
        return ((rr * 2 + sc % 2) * LEV + l) * 24 + sc // 2

    def window_at(l, rr, sc):
        return (sc // WLON) * WTOK + (l * ROWS + rr - 1) * WLON + sc % WLON

    def seen(n, r, c):
        return (r + 4 if n < 2 else r - 2), (c + 6 if n % 2 == 0 else c - 42)

    for p, n, l, r, c in pieces((range(0, 4), range(2, 6)), near, far, IN_PADS):
        t[QL if n < 2 else QL2, (l * ROWS + r) * COLS + c] = p
        rr, sc = seen(n, r, c)
        t[PXM, p] = merge_at(l, rr, sc)
        if 1 <= rr <= 6:
            t[PXW, p] = window_at(l, rr, sc)
    for l in range(LEV):
        for rr in range(1, 7):
            for sc in range(COLS):
                t[PWM, window_at(l, rr, sc)] = merge_at(l, rr, sc) - 96
                t[PMW, merge_at(l, rr, sc) - 96] = window_at(l, rr, sc)
    for p, n, l, r, c in pieces((range(0, 3), range(3, 6)), near, far, OUT_PADS):
        rr, sc = seen(n, r, c)
        t[PPO, window_at(l, rr, sc)] = p
        t[PF, p] = (l * ROWS + r) * COLS + c
    for p, n, l, r, c in pieces((range(0, 2), range(1, 3)), range(0, 21), range(21, 24), COARSE_PADS):
        t[QC if n < 2 else QC2, (l * 3 + r) * 24 + c] = p
        cr = r + 2 if n < 2 else r - 1
        cc = c + 3 if n % 2 == 0 else c - 21
        t[PC, p] = (cr * LEV + l) * 24 + cc
    for c in range(WLON):
        for j in range(WTOK):
            l2, r2, c2 = j // 72, j // 12 % 6, j % 12
            t[E0 + c, ((1 - l2) * 11 + 5 - r2) * 23 + c - c2 + 11] = j
    return t


def pick(maps, n, rows, cols, base=0):
    at = lax.broadcasted_iota(jnp.int32, (rows, cols), 0) + base
    return jnp.where(at == maps[n : n + 1, 0:cols], 1.0, 0.0).astype(BF)


def mm(a, b):
    return lax.dot_general(a, b, (((1,), (0,)), ((), ())), preferred_element_type=F32)


def mm_nt(a, b):
    return lax.dot_general(a, b, (((1,), (1,)), ((), ())), preferred_element_type=F32)


def mm_tn(a, b):
    return lax.dot_general(a, b, (((0,), (0,)), ((), ())), preferred_element_type=F32)


def layer_stats(x):
    center = x - jnp.mean(x, -1, keepdims=True)
    inverse = lax.rsqrt(jnp.mean(center * center, -1, keepdims=True) + EPS)
    return center * inverse, inverse


def norm_back(up, gain, normed, inverse):
    s = up * gain
    return inverse * (
        s - jnp.mean(s, -1, keepdims=True) - normed * jnp.mean(s * normed, -1, keepdims=True)
    )


def head_mask(h, rows):
    lane = lax.broadcasted_iota(jnp.int32, (rows, DA), 1)
    return (lane >= h * HD) & (lane < (h + 1) * HD)


def stack_heads(x):
    zero = jnp.zeros_like(x)
    return jnp.concatenate(
        [jnp.where(head_mask(h, x.shape[0]), x, zero) for h in range(HEADS)], 0
    )


def vspec():
    return pl.BlockSpec(memory_space=pltpu.VMEM)


def call(kernel, name, ins, outs, scratch=(), cid=None, smem=0, hbm=0, mib=16):
    params = dict(vmem_limit_bytes=mib << 20)
    if cid is not None:
        params.update(collective_id=cid, has_side_effects=True)
    specs = [pl.BlockSpec(memory_space=pltpu.SMEM)] * smem
    specs += [vspec()] * (len(ins) - smem - hbm) + [pl.BlockSpec(memory_space=pl.ANY)] * hbm
    return pl.pallas_call(
        kernel,
        out_shape=[jax.ShapeDtypeStruct(s, d) for s, d in outs],
        in_specs=specs,
        out_specs=[vspec()] * len(outs),
        scratch_shapes=list(scratch),
        compiler_params=pltpu.CompilerParams(**params),
        name=name,
    )(*ins)


def device(dlon, dlat, dtp):
    nlon, nlat = lax.axis_size("lon"), lax.axis_size("lat")
    return (
        lax.rem(lax.axis_index("lon") + dlon + nlon, nlon),
        lax.rem(lax.axis_index("lat") + dlat + nlat, nlat),
        lax.rem(lax.axis_index("tp") + dtp, 2),
    )


def remote(src, dst, ss, rs, n, dev):
    return pltpu.make_async_remote_copy(
        src, dst, ss.at[n], rs.at[n], device_id=dev, device_id_type=MESH
    )


class Links:
    def __init__(self, ss, rs):
        self.ss, self.rs, self.n = ss, rs, 0

    def send(self, src, dst, dev):
        c = remote(src, dst, self.ss, self.rs, self.n, dev)
        self.n += 1
        c.start()
        return c


def wait(copies):
    for c in copies:
        c.wait()


def kmain(
    pole_ref, maps, tab_ref, gain_ref, mgain_ref, lat_hbm, cg_hbm, w_hbm, proj_hbm, mw_hbm,
    rp_ref, om_ref, oq_ref, ov_ref, oa_ref,
    lat, cg, mw, wf, pf, tabs, et, bm, u, wide,
    sp, sc, pc, cc, cmt, dmo, dmp,
    xw, hn, qkv, pr, ao, y, yh, mb, dyt, mg,
    gm, dyw, do, dqkv, dst, t, gq, lp, sv, av,
    sm1, sq1, rm1, rq1, sv1, av1,
    am, aq, sm2, sq2, rm2, rq2, sv2, av2,
    bmm, bq, sm3, rm3, rq3, sv3, av3,
    cm, cq, rm4, rq4, sv4, av4, ls, ss, rs,
):
    lon, band, tp = lax.axis_index("lon"), lax.axis_index("lat"), lax.axis_index("tp")
    z, core = lax.div(lon, 2), lax.rem(lon, 2)
    yy, xx = lax.div(band, 2), lax.rem(band, 2)
    peer = device(0, 0, 1)
    core_dev = (z * 2 + 1 - core, band, tp)
    x_dev = (lon, yy * 2 + 1 - xx, tp)
    y_devs = [(lon, lax.rem(yy + k, NY) * 2 + xx, tp) for k in range(1, NY)]
    z_devs = [(lax.rem(z + k, NZ) * 2 + core, band, tp) for k in range(1, NZ)]
    near = [device(s * o, s * a, 0) for s in (1, -1) for o, a in ((1, 0), (0, 1), (1, 1))]
    partners = [peer, core_dev, x_dev] + y_devs + z_devs + near
    barrier = pltpu.get_barrier_semaphore()
    for dev in partners:
        pl.semaphore_signal(barrier, inc=1, device_id=dev, device_id_type=MESH)
    links = Links(ss, rs)
    scale = HD**-0.5
    other = 1 - tp

    loads = []
    for n, (src, into) in enumerate(
        ((lat_hbm, lat), (cg_hbm, cg), (w_hbm, wf.at[tp]), (proj_hbm, pf.at[tp]), (mw_hbm, mw))
    ):
        loads.append(pltpu.make_async_copy(src, into, ls.at[n]))
        loads[-1].start()

    nrows = pole_ref.shape[0]
    i = lax.broadcasted_iota(jnp.int32, (WTOK, WTOK), 0)
    j = lax.broadcasted_iota(jnp.int32, (WTOK, WTOK), 1)
    ri, rj = lax.rem(lax.div(i, WLON), ROWS), lax.rem(lax.div(j, WLON), ROWS)
    valid = jnp.zeros((WTOK, WTOK), jnp.int32)
    for r in range(ROWS):
        flag = pole_ref[lax.rem(band * ROWS + (r - 3 + nrows), nrows)]
        valid = jnp.where(rj == r, flag, valid)
    cut = jnp.where(band == 0, 3, 0)
    same = jnp.where(ri < cut, 1, 0) == jnp.where(rj < cut, 1, 0)
    allowed = (valid > 0) & same

    def build_bias(g):
        for l in range(LEV):
            for r in range(ROWS):
                shift = (l * 11 + r) * 23
                row = tabs[g]
                if shift:
                    row = pltpu.roll(row, 768 - shift, 1)
                for h in range(HEADS):
                    n = h * 12 + l * ROWS + r
                    u[n : n + 1, :] = row[h : h + 1, :512]
        t0 = u[...]
        hi = t0.astype(BF)
        rest = t0 - hi.astype(F32)
        mid = rest.astype(BF)
        low = (rest - mid.astype(F32)).astype(BF)
        split = jnp.concatenate([hi, mid, low], 0)
        for c in range(WLON):
            v = mm_nt(split, et[c * WTOK : (c + 1) * WTOK, :])
            v = v[0:48] + v[48:96] + v[96:144]
            wide[0, pl.ds(c, 48, stride=WLON), :] = v[:, 0:128]
            wide[1, pl.ds(c, 48, stride=WLON), :] = jnp.concatenate(
                [v[:, 128:WTOK], jnp.zeros((48, 256 - WTOK), F32)], 1
            )
        for h in range(HEADS):
            rows = slice(h * WTOK, (h + 1) * WTOK)
            both = jnp.concatenate([wide[0, rows, :], wide[1, rows, 0 : WTOK - 128]], 1)
            bm[g, rows, :] = jnp.where(allowed, both, NEG)

    tabs[tp] = jnp.zeros((8, 768), F32)
    tabs[tp, 0:HEADS, 0:NREL] = tab_ref[...]
    for c in range(WLON):
        et[c * WTOK : (c + 1) * WTOK, :] = pick(maps, E0 + c, WTOK, 512)
    build_bias(tp)

    loads[0].wait()
    loads[1].wait()
    for m, lo, hi in ((QL2, 384, 768), (QL, 336, 384)):
        sp[lo:hi, :] = mm(pick(maps, m, hi - lo, TOK, lo), lat[...]).astype(BF)
    for m, lo, hi in ((QC2, 112, 224), (QC, 96, 112)):
        sc[lo:hi, :] = mm(pick(maps, m, hi - lo, 144, lo), cg[...]).astype(BF)
    loads[2].wait()
    loads[3].wait()
    at = pl.ds(pl.multiple_of(yy * 128, 128), 128)
    pat = pl.ds(pl.multiple_of(yy * 64, 64), 64)
    pl.semaphore_wait(barrier, len(partners))
    halo = [links.send(sp.at[384:720], pc.at[384:720], device(0, 1, 0))]
    chalo = [links.send(sc.at[112:208], cc.at[112:208], device(0, 1, 0))]
    first = [
        links.send(wf.at[tp, :, at], wf.at[tp, :, at], peer),
        links.send(pf.at[tp, pat], pf.at[tp, pat], peer),
    ]
    tabc = [links.send(tabs.at[tp], tabs.at[tp], peer)]
    halo.append(links.send(sp.at[720:768], pc.at[720:768], device(1, 1, 0)))
    halo.append(links.send(sp.at[336:384], pc.at[336:384], device(1, 0, 0)))
    chalo.append(links.send(sc.at[208:224], cc.at[208:224], device(1, 1, 0)))
    chalo.append(links.send(sc.at[96:112], cc.at[96:112], device(1, 0, 0)))
    pc[0:336, :] = mm(pick(maps, QL, 336, TOK), lat[...]).astype(BF)
    cc[0:96, :] = mm(pick(maps, QC, 96, 144), cg[...]).astype(BF)
    loads[4].wait()
    wait(chalo)
    cmt[...] = mm(pick(maps, PC, 192, 224), cc[...]).astype(BF)
    for n in range(4):
        cols = slice(n * 512, (n + 1) * 512)
        dmo[:, cols] = mm_nt(cmt[...], mw[cols, :]).astype(BF)
    wait(first)
    ring = []
    for dev in y_devs:
        for ref in (wf.at[other, :, at], pf.at[other, pat]):
            ring.append(links.send(ref, ref, dev))
    wait(halo)
    dmc = [links.send(dmo, dmp, peer)]

    x = mm(pick(maps, PXW, TOK, 768), pc[...])
    xw[...] = x.astype(BF)
    normed, _ = layer_stats(x)
    hn[...] = (normed * gain_ref[...]).astype(BF)

    def forward(g):
        for n in range(3):
            qkv[g, :, n * DA : (n + 1) * DA] = mm(hn[...], wf[g, n]).astype(BF)

        def window(w, carry):
            rows = pl.ds(pl.multiple_of(w * WTOK, 16), WTOK)
            q = qkv[g, rows, 0:DA]
            k = qkv[g, rows, DA : 2 * DA]
            v = qkv[g, rows, 2 * DA : 3 * DA]
            s = mm_nt(stack_heads(q), k) * scale + bm[g]
            e = jnp.exp(s - jnp.max(s, -1, keepdims=True))
            p = e / jnp.sum(e, -1, keepdims=True)
            pr[g, w] = p
            pb = p.astype(BF)
            vs = stack_heads(v)
            o = jnp.zeros((WTOK, DA), F32)
            for h in range(HEADS):
                hs = slice(h * WTOK, (h + 1) * WTOK)
                o = o + mm(pb[hs], vs[hs])
            ao[g, rows, :] = o.astype(BF)
            return carry

        lax.fori_loop(0, NWIN, window, 0)

    forward(tp)
    wait(tabc)
    build_bias(other)
    wait(ring)
    forward(other)
    to_merge = pick(maps, PWM, TOK, TOK)
    x = mm(pick(maps, PXM, TOK, 768, 96), pc[...])
    for g in range(2):
        x = x + mm(mm(to_merge, ao[g]).astype(BF), pf[g])
    y[...] = x.astype(BF)
    yhc = [
        links.send(y.at[480:576], yh.at[0], device(0, 1, 0)),
        links.send(y.at[0:96], yh.at[1], device(0, -1, 0)),
    ]

    wait(dmc)
    mgain = mgain_ref[...]
    acc = jnp.zeros((1, 4 * D), F32)

    def slab(r, cp):
        lo = cp * 48
        if r == 0:
            return yh[0, lo : lo + 48, :]
        if r == 7:
            return yh[1, lo : lo + 48, :]
        lo += (r - 1) * 96
        return y[lo : lo + 48, :]

    for cr in (1, 2, 0, 3):
        if cr == 0:
            wait(yhc)
        slabs = [slab(2 * cr + rp, cp) for rp in (0, 1) for cp in (0, 1)]
        hat, inv = layer_stats(jnp.concatenate(slabs, 1).astype(F32))
        rows = slice(cr * 48, (cr + 1) * 48)
        dm = dmo[rows, :].astype(F32) + dmp[rows, :].astype(F32)
        if cr > 0:
            acc = acc + jnp.sum(dm * hat, 0, keepdims=True)
            mb[(cr - 1) * 48 : cr * 48, :] = (hat * mgain).astype(BF)
        dy = norm_back(dm, mgain, hat, inv).astype(BF)
        for q in range(4):
            r = 2 * cr + q // 2
            if 1 <= r <= 6:
                lo = (r - 1) * 96 + (q % 2) * 48
                dyt[lo : lo + 48, :] = dy[:, q * D : (q + 1) * D]
    mg[...] = acc

    for iz in range(NZ):
        part = mm_tn(mb[:, iz * 256 : (iz + 1) * 256], cmt[48:192, :])
        gm[iz] = part.reshape(2, NY, 32, 512)
        for iy in range(NY):
            sm1[iy, iz] = gm[iz, 1 - core, iy].astype(BF)
    m1 = [links.send(sm1, rm1, core_dev)]

    dyw[...] = mm(pick(maps, PMW, TOK, TOK), dyt[...]).astype(BF)
    for g in range(2):
        do[g] = mm_nt(dyw[...], pf[g]).astype(BF)
    dst[...] = jnp.zeros_like(dst)

    def backward(g, mine):
        def window(w, carry):
            rows = pl.ds(pl.multiple_of(w * WTOK, 16), WTOK)
            q = qkv[g, rows, 0:DA]
            k = qkv[g, rows, DA : 2 * DA]
            v = qkv[g, rows, 2 * DA : 3 * DA]
            p = pr[g, w]
            dos = stack_heads(do[g, rows, :])
            dp = mm_nt(dos, v)
            dv = mm_tn(p.astype(BF), dos)
            ds = p * (dp - jnp.sum(dp * p, -1, keepdims=True))
            if mine:
                dst[...] = dst[...] + ds
            dsb = ds.astype(BF)
            dk = mm_tn(dsb, stack_heads(q)) * scale
            ks = stack_heads(k)
            dq = jnp.zeros((WTOK, DA), F32)
            for h in range(HEADS):
                hs = slice(h * WTOK, (h + 1) * WTOK)
                dq = dq + mm(dsb[hs], ks[hs])
            dqkv[g, 0, rows, :] = (dq * scale).astype(BF)
            dqkv[g, 1, rows, :] = dk.astype(BF)
            dqkv[g, 2, rows, :] = dv.astype(BF)
            return carry

        lax.fori_loop(0, NWIN, window, 0)

    backward(tp, True)

    wait(m1)
    m2 = []
    for k in range(1, NY):
        iy = lax.rem(yy + k, NY)
        for iz in range(NZ):
            sm2[k - 1, iz] = (gm[iz, core, iy] + rm1[iy, iz].astype(F32)).astype(BF)
        m2.append(links.send(sm2.at[k - 1], rm2.at[k - 1], y_devs[k - 1]))

    for n in range(4):
        part = mm_tn(hn[...], dqkv[tp, n]) if n < 3 else mm_tn(dyw[...], ao[tp])
        gq[:, :, :, :, n * DA : (n + 1) * DA] = part.reshape(NZ, 2, NY, 8, DA)
    for iy in range(NY):
        for iz in range(0, NZ, 2):
            pair = jnp.concatenate([gq[iz, 1 - core, iy], gq[iz + 1, 1 - core, iy]], 0)
            sq1[iy, iz * 8 : iz * 8 + 16, :] = pair.astype(BF)
    q1 = [links.send(sq1, rq1, core_dev)]
    for iz in range(NZ):
        am[iz] = gm[iz, core, yy] + rm1[yy, iz].astype(F32)

    wide[0] = dst[:, 0:128]
    wide[1, :, 0 : WTOK - 128] = dst[:, 128:WTOK]
    acc = jnp.zeros((48, 512), F32)
    for c in range(WLON):
        rows = pl.ds(c, 48, stride=WLON)
        x = jnp.concatenate([wide[0, rows, :], wide[1, rows, :][:, 0 : WTOK - 128]], 1)
        hi = x.astype(BF)
        low = (x - hi.astype(F32)).astype(BF)
        v = mm(jnp.concatenate([hi, low], 0), et[c * WTOK : (c + 1) * WTOK, :])
        acc = acc + v[0:48] + v[48:96]
    t[:, 0:512] = acc
    t[:, 512:768] = jnp.zeros((48, 256), F32)
    for h in range(HEADS):
        out = jnp.zeros((1, 768), F32)
        for g in range(12):
            row = t[h * 12 + g : h * 12 + g + 1, :]
            shift = (g // ROWS * 11 + g % ROWS) * 23
            out = out + (pltpu.roll(row, shift, 1) if shift else row)
        sv[h : h + 1, :] = out
    sv[4:5, :] = mg[:, 0:768]
    sv[5:6, :] = mg[:, 768:1536]
    sv[6:7, 0:512] = mg[:, 1536:2048]
    sv[6:7, 512:768] = jnp.zeros((1, 256), F32)
    sv[7:8, :] = jnp.zeros((1, 768), F32)
    sv1[core] = sv[...]
    v1 = [links.send(sv1.at[core], sv1.at[core], core_dev)]

    backward(other, False)

    wait(q1)
    q2 = []
    for k in range(1, NY):
        iy = lax.rem(yy + k, NY)
        for iz in range(0, NZ, 2):
            pair = jnp.concatenate([gq[iz, core, iy], gq[iz + 1, core, iy]], 0)
            rows = slice(iz * 8, iz * 8 + 16)
            sq2[k - 1, rows, :] = (pair + rq1[iy, rows, :].astype(F32)).astype(BF)
        q2.append(links.send(sq2.at[k - 1], rq2.at[k - 1], y_devs[k - 1]))
    wait(v1)
    sv2[yy] = sv1[0] + sv1[1]
    v2 = [links.send(sv2.at[yy], sv2.at[yy], dev) for dev in y_devs]

    dh = jnp.zeros((TOK, D), F32)
    for g in range(2):
        for n in range(3):
            dh = dh + mm_nt(dqkv[g, n], wf[g, n])
    normed, inv = layer_stats(xw[...].astype(F32))
    av[...] = jnp.sum(dh * normed, 0, keepdims=True)
    av1[core] = av[...]
    a1 = [links.send(av1.at[core], av1.at[core], core_dev)]
    branch = norm_back(dh, gain_ref[...], normed, inv).astype(BF)
    lg = (dyw[...].astype(F32) + branch.astype(F32)).astype(BF)
    lp[...] = mm(pick(maps, PPO, 608, TOK), lg).astype(BF)
    ro = [
        links.send(lp.at[304:560], rp_ref.at[304:560], device(0, -1, 0)),
        links.send(lp.at[256:304], rp_ref.at[256:304], device(-1, 0, 0)),
        links.send(lp.at[560:608], rp_ref.at[560:608], device(-1, -1, 0)),
    ]
    wait(a1)
    av2[yy] = av1[0] + av1[1]
    a2 = [links.send(av2.at[yy], av2.at[yy], dev) for dev in y_devs]
    rp_ref[0:256, :] = lp[0:256, :]

    wait(m2)
    for iz in range(NZ):
        acc = am[iz]
        for k in range(NY - 1):
            acc = acc + rm2[k, iz].astype(F32)
        bmm[iz] = acc
    m3 = []
    for k in range(1, NZ):
        sm3[k - 1] = bmm[lax.rem(z + k, NZ)].astype(BF)
        m3.append(links.send(sm3.at[k - 1], rm3.at[k - 1], z_devs[k - 1]))

    for iz in range(0, NZ, 2):
        pair = jnp.concatenate([gq[iz, core, yy], gq[iz + 1, core, yy]], 0)
        rows = slice(iz * 8, iz * 8 + 16)
        aq[rows, :] = pair + rq1[yy, rows, :].astype(F32)
    wait(q2)
    acc = aq[...]
    for k in range(NY - 1):
        acc = acc + rq2[k].astype(F32)
    for iz in range(NZ):
        bq[iz] = acc[iz * 8 : iz * 8 + 8]
    q3 = [
        links.send(bq.at[lax.rem(z + k, NZ)], rq3.at[k - 1], z_devs[k - 1])
        for k in range(1, NZ)
    ]
    wait(v2)
    sv3[z] = sv2[0] + sv2[1] + sv2[2] + sv2[3]
    v3 = [links.send(sv3.at[z], sv3.at[z], dev) for dev in z_devs]
    wait(a2)
    av3[z] = av2[0] + av2[1] + av2[2] + av2[3]
    a3 = [links.send(av3.at[z], av3.at[z], dev) for dev in z_devs]

    wait(m3)
    acc = bmm[z]
    for k in range(NZ - 1):
        acc = acc + rm3[k].astype(F32)
    cm[0] = acc[0:16]
    cm[1] = acc[16:32]
    m4 = [links.send(cm.at[1 - xx], rm4, x_dev)]
    wait(q3)
    acc = bq[z]
    for k in range(NZ - 1):
        acc = acc + rq3[k]
    cq[...] = acc
    q4 = [links.send(cq, rq4, x_dev)]
    wait(v3)
    acc = sv3[0]
    for k in range(1, NZ):
        acc = acc + sv3[k]
    sv4[xx] = acc
    v4 = [links.send(sv4.at[xx], sv4.at[xx], x_dev)]
    wait(a3)
    acc = av3[0]
    for k in range(1, NZ):
        acc = acc + av3[k]
    av4[xx] = acc
    v4.append(links.send(av4.at[xx], av4.at[xx], x_dev))
    wait(m4)
    om_ref[...] = cm[xx] + rm4[...]
    wait(q4)
    oq_ref[...] = cq[...] + rq4[...]
    wait(v4)
    ov_ref[...] = sv4[0] + sv4[1]
    oa_ref[...] = av4[0] + av4[1]
    wait(ro)


def kend(
    maps, rp_ref, om_ref, oq_ref, ov_ref, oa_ref, lg_ref, ag_ref, gw_ref, gp_ref, gb_ref, mg_ref,
    gm_ref,
):
    xx = lax.rem(lax.axis_index("lat"), 2)
    lg_ref[...] = mm(pick(maps, PF, TOK, 608), rp_ref[...]).astype(BF)
    gm_ref[...] = om_ref[...]
    mine = jnp.where(xx == 0, oq_ref[0:4, :], oq_ref[4:8, :])
    for n in range(3):
        gw_ref[n] = mine[:, n * DA : (n + 1) * DA]
    gp_ref[...] = mine[:, 3 * DA :]
    gb_ref[...] = ov_ref[0:HEADS, 0:NREL]
    mg_ref[:, 0:768] = ov_ref[4:5, :]
    mg_ref[:, 768:1536] = ov_ref[5:6, :]
    mg_ref[:, 1536:2048] = ov_ref[6:7, 0:512]
    ag_ref[...] = oa_ref[...]


def local(
    latent, pole_mask, attn_gain, qkv_weight, proj_weight, rel_bias, merge_gain, merge_weight,
    coarse_grad,
):
    maps = jnp.asarray(index_maps())
    dma = pltpu.SemaphoreType.DMA
    vm = pltpu.VMEM
    nb = HEADS * WTOK
    nv, na = (8, 768), (1, D)
    sends = 80
    rp, om, oq, ov, oa = call(
        kmain, "sublayer_backward",
        [
            pole_mask, maps, rel_bias, attn_gain.reshape(1, D), merge_gain.reshape(1, 4 * D),
            latent.reshape(TOK, D), coarse_grad.reshape(144, 512), qkv_weight.transpose(1, 0, 2),
            proj_weight, merge_weight,
        ],
        [((608, D), BF), ((16, 512), F32), ((8, 1024), F32), (nv, F32), (na, F32)],
        [
            vm((TOK, D), BF), vm((144, 512), BF), vm((4 * D, 512), BF), vm((2, 3, D, DA), BF),
            vm((2, DA, D), BF), vm((2, 8, 768), F32), vm((WLON * WTOK, 512), BF),
            vm((2, nb, WTOK), F32), vm((48, 512), F32), vm((2, nb, 128), F32),
            vm((768, D), BF), vm((224, 512), BF), vm((768, D), BF), vm((224, 512), BF),
            vm((192, 512), BF), vm((192, 4 * D), BF), vm((192, 4 * D), BF),
            vm((TOK, D), BF), vm((TOK, D), BF), vm((2, TOK, 3 * DA), BF),
            vm((2, NWIN, nb, WTOK), F32), vm((2, TOK, DA), BF), vm((TOK, D), BF),
            vm((2, 96, D), BF), vm((144, 4 * D), BF), vm((TOK, D), BF), vm((1, 4 * D), F32),
            vm((NZ, 2, NY, 32, 512), F32), vm((TOK, D), BF), vm((2, TOK, DA), BF),
            vm((2, 3, TOK, DA), BF), vm((nb, WTOK), F32), vm((48, 768), F32),
            vm((NZ, 2, NY, 8, 1024), F32), vm((608, D), BF), vm(nv, F32), vm(na, F32),
            vm((NY, NZ, 32, 512), BF), vm((NY, 64, 1024), BF),
            vm((NY, NZ, 32, 512), BF), vm((NY, 64, 1024), BF), vm((2,) + nv, F32),
            vm((2,) + na, F32),
            vm((NZ, 32, 512), F32), vm((64, 1024), F32),
            vm((NY - 1, NZ, 32, 512), BF), vm((NY - 1, 64, 1024), BF),
            vm((NY - 1, NZ, 32, 512), BF), vm((NY - 1, 64, 1024), BF), vm((NY,) + nv, F32),
            vm((NY,) + na, F32),
            vm((NZ, 32, 512), F32), vm((NZ, 8, 1024), F32),
            vm((NZ - 1, 32, 512), BF), vm((NZ - 1, 32, 512), BF),
            vm((NZ - 1, 8, 1024), F32), vm((NZ,) + nv, F32), vm((NZ,) + na, F32),
            vm((2, 16, 512), F32), vm((8, 1024), F32),
            vm((16, 512), F32), vm((8, 1024), F32), vm((2,) + nv, F32), vm((2,) + na, F32),
            dma((5,)), dma((sends,)), dma((sends,)),
        ],
        cid=1, mib=58, smem=1, hbm=5,
    )
    lg, ag, gw, gp, gb, mgg, gmm = call(
        kend, "finish", [maps, rp, om, oq, ov, oa],
        [
            ((TOK, D), BF), ((1, D), F32), ((3, 4, DA), F32), ((4, DA), F32),
            ((HEADS, NREL), F32), ((1, 4 * D), F32), ((16, 512), F32),
        ],
        mib=8,
    )
    return (
        lg.reshape(latent.shape),
        ag.reshape(D),
        gw.transpose(1, 0, 2),
        gp.T,
        gb,
        mgg.reshape(4 * D),
        gmm,
    )


def solution(mesh):
    placed = (
        P(None, "lat", "lon", None),
        P(),
        P(),
        P(None, None, "tp"),
        P("tp", None),
        P("tp", None),
        P(),
        P(None, "tp"),
        P(None, "lat", "lon", "tp"),
    )
    return jax.shard_map(
        local,
        mesh=mesh,
        in_specs=placed,
        out_specs=(
            P(None, "lat", "lon", None),
            P(),
            P(("lon", "lat"), None, "tp"),
            P("tp", ("lon", "lat")),
            P("tp", None),
            P(),
            P(("lon", "lat"), "tp"),
        ),
        check_vma=False,
    )
```

time: 134 us -> 111 us (0.83)
  Pallas kernels: 118 us -> 105 us
  local copies, waits for them, and re-layouts: 9.79 us -> 3.99 us
  waiting for transfers between devices: 3.19 us -> 0 us
    pallas_call x6 -> x2, Pallas kernels: 118 us -> 105 us  [call(): pl.pallas_call(kernel, out_shape=[jax.ShapeDtypeStruct(s, d) for s, d in...]
    unnamed x26 -> x12, local copies, waits for them, and re-layouts: 9.79 us -> 3.99 us
    ppermute x1 -> x0, waiting for transfers between devices: 3.19 us -> none  [local(): dmp = lax.ppermute(dmo, 'tp', [(0, 1), (1, 0)])]
  transfers between devices with their start and end apart: 1 -> 0, of which waited for: 1 -> 0; matrix products, arithmetic and copies ran while one was open for 0% -> 0% of each run, Pallas kernels for 8% -> 0%
where the time goes in v3:
time: 111 us; the launch traced here: 110 us
  Pallas kernels  105 us (95%)
  local copies, waits for them, and re-layouts  3.99 us (4%)
    pallas_call x2, Pallas kernels, call(): pl.pallas_call(kernel, out_shape=[jax.ShapeDtypeStruct(s, d) for s, d in...  105 us
    unnamed x12, local copies, waits for them, and re-layouts  3.99 us

profile of v3, /device:TPU:2, one launch (start us, length us, event | category | flops | bytes accessed | tf_op | source)
XLA Modules:
  0.0 109.6 jit_solution(8699350567827715233)
XLA Ops:
  0.6 0.0 copy-start.1
  0.6 103.5 %sublayer_backward.1 = (bf16[608,512]{1,0:T(8,128)(2,1)}, f32[16,512]{1,0:T(8,128)}, f32[8,1024]{1,0:T(8,128)}, f32[8,768]{1,0:T(8,128)}, f32[1,512]{1,0:T(1,128)}) custom-call(s32[48]{0:T(128)} %pole_ref.1, s32[24,768]{1,0:T(8,128)} %constant.2.clone.maps, f32[4,759]{1,0:T(4,128)} %tab_ref.1, f32[1,512]{1,0:T(1,128)} %bitcast.14, f32[1,2048]{1,0:T(1,128)} %bitcast.13, ...), custom_call_target="tpu_custom_call" | custom-call | tf_op jit(solution)/shard_map/sublayer_backward/pallas_call | solution.py:143
  104.2 0.0 copy-done.1
  104.2 0.0 copy-start
  104.2 1.1 copy-done
  105.3 0.0 copy-start.2
  105.3 0.8 copy-done.2
  106.0 0.0 copy-start.3
  106.0 0.8 copy-done.3
  106.8 0.0 copy-start.4
  106.8 0.7 copy-done.4
  107.5 0.0 copy-start.5
  107.5 0.7 copy-done.5
  108.2 1.4 %finish.1 = (bf16[576,512]{1,0:T(8,128)(2,1)}, f32[1,512]{1,0:T(1,128)}, f32[3,4,256]{2,1,0:T(4,128)}, f32[4,256]{1,0:T(4,128)}, f32[4,759]{1,0:T(4,128)}, /*index=5*/f32[1,2048]{1,0:T(1,128)}, f32[16,512]{1,0:T(8,128)}) custom-call(s32[24,768]{1,0:T(8,128)S(1)} %copy-done.1, bf16[608,512]{1,0:T(8,128)(2,1)S(1)} %copy-done, f32[16,512]{1,0:T(8,128)S(1)} %copy-done.2, ...), custom_call_target="tpu_custom_call" | custom-call | tf_op jit(solution)/shard_map/finish/pallas_call | solution.py:143
Async XLA Ops:
  0.6 103.5 %copy-start.1 = (s32[24,768]{1,0:T(8,128)S(1)}, s32[24,768]{1,0:T(8,128)}, u32[]{:S(2)}) copy-start(s32[24,768]{1,0:T(8,128)} %constant.2.clone.maps) | copy-start | bytes 221188
  104.2 1.1 copy-start
  105.3 0.8 copy-start.2
  106.0 0.8 copy-start.3
  106.8 0.7 copy-start.4
  107.5 0.7 copy-start.5

commit v4 on v3

--- a/solution.py
+++ b/solution.py
@@ -26,9 +26,8 @@
 NZ, NY = 8, 4
 
 
-(QL, QL2, QC, QC2, PC, PXM, PXW, PWM, PMW, PPO, PF, E0) = range(12)
+(QL, QL2, QC, QC2, PC, PXM, PXW, PWM, PMW, PPO, PF, FP, E0) = range(13)
 MAPW = 768
-IN_PADS = (336, 48, 336, 48)
 OUT_PADS = (256, 48, 256, 48)
 COARSE_PADS = (96, 16, 96, 16)
 
@@ -49,7 +48,7 @@
 
 @functools.lru_cache(None)
 def index_maps():
-    t = np.full((24, MAPW), -1, np.int32)
+    t = np.full((32, MAPW), -1, np.int32)
     near, far = range(0, 42), range(42, 48)
 
     def merge_at(l, rr, sc):
@@ -61,12 +60,6 @@
     def seen(n, r, c):
         return (r + 4 if n < 2 else r - 2), (c + 6 if n % 2 == 0 else c - 42)
 
-    for p, n, l, r, c in pieces((range(0, 4), range(2, 6)), near, far, IN_PADS):
-        t[QL if n < 2 else QL2, (l * ROWS + r) * COLS + c] = p
-        rr, sc = seen(n, r, c)
-        t[PXM, p] = merge_at(l, rr, sc)
-        if 1 <= rr <= 6:
-            t[PXW, p] = window_at(l, rr, sc)
     for l in range(LEV):
         for rr in range(1, 7):
             for sc in range(COLS):
@@ -74,6 +67,9 @@
                 t[PMW, merge_at(l, rr, sc) - 96] = window_at(l, rr, sc)
     for p, n, l, r, c in pieces((range(0, 3), range(3, 6)), near, far, OUT_PADS):
         rr, sc = seen(n, r, c)
+        t[QL if n < 2 else QL2, (l * ROWS + r) * COLS + c] = p
+        t[PXM, p] = merge_at(l, rr, sc) - 96
+        t[PXW, p] = window_at(l, rr, sc)
         t[PPO, window_at(l, rr, sc)] = p
         t[PF, p] = (l * ROWS + r) * COLS + c
     for p, n, l, r, c in pieces((range(0, 2), range(1, 3)), range(0, 21), range(21, 24), COARSE_PADS):
@@ -81,6 +77,8 @@
         cr = r + 2 if n < 2 else r - 1
         cc = c + 3 if n % 2 == 0 else c - 21
         t[PC, p] = (cr * LEV + l) * 24 + cc
+    order = np.arange(D).reshape(NZ, 2, NY, 2, 4).transpose(1, 3, 2, 0, 4)
+    t[FP, 0:D] = order.reshape(-1)
     for c in range(WLON):
         for j in range(WTOK):
             l2, r2, c2 = j // 72, j // 12 % 6, j % 12
@@ -187,12 +185,12 @@
     rp_ref, om_ref, oq_ref, ov_ref, oa_ref,
     lat, cg, mw, wf, pf, tabs, et, bm, u, wide,
     sp, sc, pc, cc, cmt, dmo, dmp,
-    xw, hn, qkv, pr, ao, y, yh, mb, dyt, mg,
-    gm, dyw, do, dqkv, dst, t, gq, lp, sv, av,
+    xw, hn, hnp, qkv, pr, ao, y, yh, mb, dyt, mg,
+    gm, dyw, dyp, do, dqkv, dst, t, gq, lp, sv, av,
     sm1, sq1, rm1, rq1, sv1, av1,
-    am, aq, sm2, sq2, rm2, rq2, sv2, av2,
-    bmm, bq, sm3, rm3, rq3, sv3, av3,
-    cm, cq, rm4, rq4, sv4, av4, ls, ss, rs,
+    am, sm2, rm2, bmm, sm3, rm3, cm, rm4,
+    aq, sq2, rq2, bq, sq3, rq3, cq, rq4,
+    sv2, av2, sv3, av3, sv4, av4, ls, ss, rs,
 ):
     lon, band, tp = lax.axis_index("lon"), lax.axis_index("lat"), lax.axis_index("tp")
     z, core = lax.div(lon, 2), lax.rem(lon, 2)
@@ -260,49 +258,54 @@
 
     tabs[tp] = jnp.zeros((8, 768), F32)
     tabs[tp, 0:HEADS, 0:NREL] = tab_ref[...]
-    for c in range(WLON):
-        et[c * WTOK : (c + 1) * WTOK, :] = pick(maps, E0 + c, WTOK, 512)
-    build_bias(tp)
-
     loads[0].wait()
     loads[1].wait()
-    for m, lo, hi in ((QL2, 384, 768), (QL, 336, 384)):
+    for m, lo, hi in ((QL2, 304, 608), (QL, 256, 304)):
         sp[lo:hi, :] = mm(pick(maps, m, hi - lo, TOK, lo), lat[...]).astype(BF)
     for m, lo, hi in ((QC2, 112, 224), (QC, 96, 112)):
         sc[lo:hi, :] = mm(pick(maps, m, hi - lo, 144, lo), cg[...]).astype(BF)
     loads[2].wait()
     loads[3].wait()
-    at = pl.ds(pl.multiple_of(yy * 128, 128), 128)
-    pat = pl.ds(pl.multiple_of(yy * 64, 64), 64)
+    at = pl.ds(pl.multiple_of(core * 256 + yy * 64, 64), 64)
+    pat = pl.ds(pl.multiple_of(core * 128 + yy * 32, 32), 32)
+    half = pl.ds(pl.multiple_of(core * 256, 256), 256)
+    phalf = pl.ds(pl.multiple_of(core * 128, 128), 128)
     pl.semaphore_wait(barrier, len(partners))
-    halo = [links.send(sp.at[384:720], pc.at[384:720], device(0, 1, 0))]
     chalo = [links.send(sc.at[112:208], cc.at[112:208], device(0, 1, 0))]
+    halo = [links.send(sp.at[304:560], pc.at[304:560], device(0, 1, 0))]
+    chalo.append(links.send(sc.at[208:224], cc.at[208:224], device(1, 1, 0)))
+    chalo.append(links.send(sc.at[96:112], cc.at[96:112], device(1, 0, 0)))
     first = [
         links.send(wf.at[tp, :, at], wf.at[tp, :, at], peer),
         links.send(pf.at[tp, pat], pf.at[tp, pat], peer),
     ]
+    halo.append(links.send(sp.at[560:608], pc.at[560:608], device(1, 1, 0)))
+    halo.append(links.send(sp.at[256:304], pc.at[256:304], device(1, 0, 0)))
     tabc = [links.send(tabs.at[tp], tabs.at[tp], peer)]
-    halo.append(links.send(sp.at[720:768], pc.at[720:768], device(1, 1, 0)))
-    halo.append(links.send(sp.at[336:384], pc.at[336:384], device(1, 0, 0)))
-    chalo.append(links.send(sc.at[208:224], cc.at[208:224], device(1, 1, 0)))
-    chalo.append(links.send(sc.at[96:112], cc.at[96:112], device(1, 0, 0)))
-    pc[0:336, :] = mm(pick(maps, QL, 336, TOK), lat[...]).astype(BF)
+    pc[0:256, :] = mm(pick(maps, QL, 256, TOK), lat[...]).astype(BF)
     cc[0:96, :] = mm(pick(maps, QC, 96, 144), cg[...]).astype(BF)
+    for c in range(WLON):
+        et[c * WTOK : (c + 1) * WTOK, :] = pick(maps, E0 + c, WTOK, 512)
     loads[4].wait()
     wait(chalo)
     cmt[...] = mm(pick(maps, PC, 192, 224), cc[...]).astype(BF)
     for n in range(4):
         cols = slice(n * 512, (n + 1) * 512)
         dmo[:, cols] = mm_nt(cmt[...], mw[cols, :]).astype(BF)
+    dmc = [links.send(dmo.at[48:144], dmp.at[48:144], peer)]
+    dmh = [
+        links.send(dmo.at[0:48], dmp.at[0:48], peer),
+        links.send(dmo.at[144:192], dmp.at[144:192], peer),
+    ]
     wait(first)
     ring = []
     for dev in y_devs:
         for ref in (wf.at[other, :, at], pf.at[other, pat]):
             ring.append(links.send(ref, ref, dev))
+    build_bias(tp)
     wait(halo)
-    dmc = [links.send(dmo, dmp, peer)]
-
-    x = mm(pick(maps, PXW, TOK, 768), pc[...])
+
+    x = mm(pick(maps, PXW, TOK, 608), pc[...])
     xw[...] = x.astype(BF)
     normed, _ = layer_stats(x)
     hn[...] = (normed * gain_ref[...]).astype(BF)
@@ -332,12 +335,16 @@
         lax.fori_loop(0, NWIN, window, 0)
 
     forward(tp)
+    features = pick(maps, FP, D, D)
+    hnp[...] = mm(hn[...], features).astype(BF)
+    wait(ring)
+    pair = [links.send(r, r, core_dev) for r in (wf.at[other, :, half], pf.at[other, phalf])]
     wait(tabc)
     build_bias(other)
-    wait(ring)
+    wait(pair)
     forward(other)
     to_merge = pick(maps, PWM, TOK, TOK)
-    x = mm(pick(maps, PXM, TOK, 768, 96), pc[...])
+    x = mm(pick(maps, PXM, TOK, 608), pc[...])
     for g in range(2):
         x = x + mm(mm(to_merge, ao[g]).astype(BF), pf[g])
     y[...] = x.astype(BF)
@@ -362,6 +369,7 @@
     for cr in (1, 2, 0, 3):
         if cr == 0:
             wait(yhc)
+            wait(dmh)
         slabs = [slab(2 * cr + rp, cp) for rp in (0, 1) for cp in (0, 1)]
         hat, inv = layer_stats(jnp.concatenate(slabs, 1).astype(F32))
         rows = slice(cr * 48, (cr + 1) * 48)
@@ -389,7 +397,7 @@
         do[g] = mm_nt(dyw[...], pf[g]).astype(BF)
     dst[...] = jnp.zeros_like(dst)
 
-    def backward(g, mine):
+    def backward(g, mine, lo=0, hi=NWIN):
         def window(w, carry):
             rows = pl.ds(pl.multiple_of(w * WTOK, 16), WTOK)
             q = qkv[g, rows, 0:DA]
@@ -414,9 +422,9 @@
             dqkv[g, 2, rows, :] = dv.astype(BF)
             return carry
 
-        lax.fori_loop(0, NWIN, window, 0)
-
-    backward(tp, True)
+        lax.fori_loop(lo, hi, window, 0)
+
+    backward(tp, True, 0, 1)
 
     wait(m1)
     m2 = []
@@ -426,13 +434,13 @@
             sm2[k - 1, iz] = (gm[iz, core, iy] + rm1[iy, iz].astype(F32)).astype(BF)
         m2.append(links.send(sm2.at[k - 1], rm2.at[k - 1], y_devs[k - 1]))
 
+    backward(tp, True, 1)
+
+    dyp[...] = mm(dyw[...], features).astype(BF)
     for n in range(4):
-        part = mm_tn(hn[...], dqkv[tp, n]) if n < 3 else mm_tn(dyw[...], ao[tp])
-        gq[:, :, :, :, n * DA : (n + 1) * DA] = part.reshape(NZ, 2, NY, 8, DA)
-    for iy in range(NY):
-        for iz in range(0, NZ, 2):
-            pair = jnp.concatenate([gq[iz, 1 - core, iy], gq[iz + 1, 1 - core, iy]], 0)
-            sq1[iy, iz * 8 : iz * 8 + 16, :] = pair.astype(BF)
+        part = mm_tn(hnp[...], dqkv[tp, n]) if n < 3 else mm_tn(dyp[...], ao[tp])
+        gq[:, :, :, :, n * DA : (n + 1) * DA] = part.reshape(2, 2, NY, 32, DA)
+    sq1[...] = gq[1 - core].astype(BF)
     q1 = [links.send(sq1, rq1, core_dev)]
     for iz in range(NZ):
         am[iz] = gm[iz, core, yy] + rm1[yy, iz].astype(F32)
@@ -464,20 +472,34 @@
     sv1[core] = sv[...]
     v1 = [links.send(sv1.at[core], sv1.at[core], core_dev)]
 
+    wait(q1)
+    sq2[...] = (gq[core, 1 - xx] + rq1[1 - xx].astype(F32)).astype(BF)
+    q2 = [links.send(sq2, rq2, x_dev)]
+    aq[...] = gq[core, xx] + rq1[xx].astype(F32)
+    wait(v1)
+    sv2[z] = sv1[0] + sv1[1]
+    v2 = [links.send(sv2.at[z], sv2.at[z], dev) for dev in z_devs]
+
     backward(other, False)
 
-    wait(q1)
-    q2 = []
+    wait(q2)
+    q3 = []
     for k in range(1, NY):
         iy = lax.rem(yy + k, NY)
-        for iz in range(0, NZ, 2):
-            pair = jnp.concatenate([gq[iz, core, iy], gq[iz + 1, core, iy]], 0)
-            rows = slice(iz * 8, iz * 8 + 16)
-            sq2[k - 1, rows, :] = (pair + rq1[iy, rows, :].astype(F32)).astype(BF)
-        q2.append(links.send(sq2.at[k - 1], rq2.at[k - 1], y_devs[k - 1]))
-    wait(v1)
-    sv2[yy] = sv1[0] + sv1[1]
-    v2 = [links.send(sv2.at[yy], sv2.at[yy], dev) for dev in y_devs]
+        sq3[k - 1] = (aq[iy] + rq2[iy].astype(F32)).astype(BF)
+        q3.append(links.send(sq3.at[k - 1], rq3.at[k - 1], y_devs[k - 1]))
+    bq[...] = aq[yy] + rq2[yy].astype(F32)
+
+    wait(m2)
+    for iz in range(NZ):
+        acc = am[iz]
+        for k in range(NY - 1):
+            acc = acc + rm2[k, iz].astype(F32)
+        bmm[iz] = acc
+    m3 = []
+    for k in range(1, NZ):
+        sm3[k - 1] = bmm[lax.rem(z + k, NZ)].astype(BF)
+        m3.append(links.send(sm3.at[k - 1], rm3.at[k - 1], z_devs[k - 1]))
 
     dh = jnp.zeros((TOK, D), F32)
     for g in range(2):
@@ -495,42 +517,34 @@
         links.send(lp.at[256:304], rp_ref.at[256:304], device(-1, 0, 0)),
         links.send(lp.at[560:608], rp_ref.at[560:608], device(-1, -1, 0)),
     ]
+    rp_ref[0:256, :] = lp[0:256, :]
+    wait(v2)
+    acc = sv2[0]
+    for k in range(1, NZ):
+        acc = acc + sv2[k]
+    sv3[xx] = acc
+    v3 = [links.send(sv3.at[xx], sv3.at[xx], x_dev)]
     wait(a1)
-    av2[yy] = av1[0] + av1[1]
-    a2 = [links.send(av2.at[yy], av2.at[yy], dev) for dev in y_devs]
-    rp_ref[0:256, :] = lp[0:256, :]
-
-    wait(m2)
+    av2[xx] = av1[0] + av1[1]
+    a2 = [links.send(av2.at[xx], av2.at[xx], x_dev)]
+
+    wait(q3)
+    acc = bq[...]
+    for k in range(NY - 1):
+        acc = acc + rq3[k].astype(F32)
     for iz in range(NZ):
-        acc = am[iz]
-        for k in range(NY - 1):
-            acc = acc + rm2[k, iz].astype(F32)
-        bmm[iz] = acc
-    m3 = []
+        rows = slice(iz * 4, iz * 4 + 4)
+        cq[iz] = jnp.concatenate([acc[rows, 0:512], acc[rows, 512:1024]], 0)
+    q4 = []
     for k in range(1, NZ):
-        sm3[k - 1] = bmm[lax.rem(z + k, NZ)].astype(BF)
-        m3.append(links.send(sm3.at[k - 1], rm3.at[k - 1], z_devs[k - 1]))
-
-    for iz in range(0, NZ, 2):
-        pair = jnp.concatenate([gq[iz, core, yy], gq[iz + 1, core, yy]], 0)
-        rows = slice(iz * 8, iz * 8 + 16)
-        aq[rows, :] = pair + rq1[yy, rows, :].astype(F32)
-    wait(q2)
-    acc = aq[...]
-    for k in range(NY - 1):
-        acc = acc + rq2[k].astype(F32)
-    for iz in range(NZ):
-        bq[iz] = acc[iz * 8 : iz * 8 + 8]
-    q3 = [
-        links.send(bq.at[lax.rem(z + k, NZ)], rq3.at[k - 1], z_devs[k - 1])
-        for k in range(1, NZ)
-    ]
-    wait(v2)
-    sv3[z] = sv2[0] + sv2[1] + sv2[2] + sv2[3]
-    v3 = [links.send(sv3.at[z], sv3.at[z], dev) for dev in z_devs]
+        q4.append(links.send(cq.at[lax.rem(z + k, NZ)], rq4.at[k - 1], z_devs[k - 1]))
+
     wait(a2)
-    av3[z] = av2[0] + av2[1] + av2[2] + av2[3]
-    a3 = [links.send(av3.at[z], av3.at[z], dev) for dev in z_devs]
+    av3[yy] = av2[0] + av2[1]
+    a3 = [links.send(av3.at[yy], av3.at[yy], dev) for dev in y_devs]
+    wait(v3)
+    sv4[yy] = sv3[0] + sv3[1]
+    v4 = [links.send(sv4.at[yy], sv4.at[yy], dev) for dev in y_devs]
 
     wait(m3)
     acc = bmm[z]
@@ -539,31 +553,23 @@
     cm[0] = acc[0:16]
     cm[1] = acc[16:32]
     m4 = [links.send(cm.at[1 - xx], rm4, x_dev)]
-    wait(q3)
-    acc = bq[z]
-    for k in range(NZ - 1):
-        acc = acc + rq3[k]
-    cq[...] = acc
-    q4 = [links.send(cq, rq4, x_dev)]
-    wait(v3)
-    acc = sv3[0]
-    for k in range(1, NZ):
-        acc = acc + sv3[k]
-    sv4[xx] = acc
-    v4 = [links.send(sv4.at[xx], sv4.at[xx], x_dev)]
     wait(a3)
-    acc = av3[0]
-    for k in range(1, NZ):
-        acc = acc + av3[k]
-    av4[xx] = acc
-    v4.append(links.send(av4.at[xx], av4.at[xx], x_dev))
+    av4[z] = av3[0] + av3[1] + av3[2] + av3[3]
+    a4 = [links.send(av4.at[z], av4.at[z], dev) for dev in z_devs]
     wait(m4)
     om_ref[...] = cm[xx] + rm4[...]
     wait(q4)
-    oq_ref[...] = cq[...] + rq4[...]
+    acc = cq[z]
+    for k in range(NZ - 1):
+        acc = acc + rq4[k]
+    oq_ref[...] = acc
     wait(v4)
-    ov_ref[...] = sv4[0] + sv4[1]
-    oa_ref[...] = av4[0] + av4[1]
+    ov_ref[...] = sv4[0] + sv4[1] + sv4[2] + sv4[3]
+    wait(a4)
+    acc = av4[0]
+    for k in range(1, NZ):
+        acc = acc + av4[k]
+    oa_ref[...] = acc
     wait(ro)
 
 
@@ -571,13 +577,12 @@
     maps, rp_ref, om_ref, oq_ref, ov_ref, oa_ref, lg_ref, ag_ref, gw_ref, gp_ref, gb_ref, mg_ref,
     gm_ref,
 ):
-    xx = lax.rem(lax.axis_index("lat"), 2)
     lg_ref[...] = mm(pick(maps, PF, TOK, 608), rp_ref[...]).astype(BF)
     gm_ref[...] = om_ref[...]
-    mine = jnp.where(xx == 0, oq_ref[0:4, :], oq_ref[4:8, :])
-    for n in range(3):
-        gw_ref[n] = mine[:, n * DA : (n + 1) * DA]
-    gp_ref[...] = mine[:, 3 * DA :]
+    gw_ref[0] = oq_ref[0:4, 0:DA]
+    gw_ref[1] = oq_ref[0:4, DA : 2 * DA]
+    gw_ref[2] = oq_ref[4:8, 0:DA]
+    gp_ref[...] = oq_ref[4:8, DA : 2 * DA]
     gb_ref[...] = ov_ref[0:HEADS, 0:NREL]
     mg_ref[:, 0:768] = ov_ref[4:5, :]
     mg_ref[:, 768:1536] = ov_ref[5:6, :]
@@ -602,31 +607,31 @@
             latent.reshape(TOK, D), coarse_grad.reshape(144, 512), qkv_weight.transpose(1, 0, 2),
             proj_weight, merge_weight,
         ],
-        [((608, D), BF), ((16, 512), F32), ((8, 1024), F32), (nv, F32), (na, F32)],
+        [((608, D), BF), ((16, 512), F32), ((8, 512), F32), (nv, F32), (na, F32)],
         [
             vm((TOK, D), BF), vm((144, 512), BF), vm((4 * D, 512), BF), vm((2, 3, D, DA), BF),
             vm((2, DA, D), BF), vm((2, 8, 768), F32), vm((WLON * WTOK, 512), BF),
             vm((2, nb, WTOK), F32), vm((48, 512), F32), vm((2, nb, 128), F32),
-            vm((768, D), BF), vm((224, 512), BF), vm((768, D), BF), vm((224, 512), BF),
+            vm((608, D), BF), vm((224, 512), BF), vm((608, D), BF), vm((224, 512), BF),
             vm((192, 512), BF), vm((192, 4 * D), BF), vm((192, 4 * D), BF),
-            vm((TOK, D), BF), vm((TOK, D), BF), vm((2, TOK, 3 * DA), BF),
+            vm((TOK, D), BF), vm((TOK, D), BF), vm((TOK, D), BF), vm((2, TOK, 3 * DA), BF),
             vm((2, NWIN, nb, WTOK), F32), vm((2, TOK, DA), BF), vm((TOK, D), BF),
             vm((2, 96, D), BF), vm((144, 4 * D), BF), vm((TOK, D), BF), vm((1, 4 * D), F32),
-            vm((NZ, 2, NY, 32, 512), F32), vm((TOK, D), BF), vm((2, TOK, DA), BF),
+            vm((NZ, 2, NY, 32, 512), F32), vm((TOK, D), BF), vm((TOK, D), BF),
+            vm((2, TOK, DA), BF),
             vm((2, 3, TOK, DA), BF), vm((nb, WTOK), F32), vm((48, 768), F32),
-            vm((NZ, 2, NY, 8, 1024), F32), vm((608, D), BF), vm(nv, F32), vm(na, F32),
-            vm((NY, NZ, 32, 512), BF), vm((NY, 64, 1024), BF),
-            vm((NY, NZ, 32, 512), BF), vm((NY, 64, 1024), BF), vm((2,) + nv, F32),
+            vm((2, 2, NY, 32, 1024), F32), vm((608, D), BF), vm(nv, F32), vm(na, F32),
+            vm((NY, NZ, 32, 512), BF), vm((2, NY, 32, 1024), BF),
+            vm((NY, NZ, 32, 512), BF), vm((2, NY, 32, 1024), BF), vm((2,) + nv, F32),
             vm((2,) + na, F32),
-            vm((NZ, 32, 512), F32), vm((64, 1024), F32),
-            vm((NY - 1, NZ, 32, 512), BF), vm((NY - 1, 64, 1024), BF),
-            vm((NY - 1, NZ, 32, 512), BF), vm((NY - 1, 64, 1024), BF), vm((NY,) + nv, F32),
-            vm((NY,) + na, F32),
-            vm((NZ, 32, 512), F32), vm((NZ, 8, 1024), F32),
-            vm((NZ - 1, 32, 512), BF), vm((NZ - 1, 32, 512), BF),
-            vm((NZ - 1, 8, 1024), F32), vm((NZ,) + nv, F32), vm((NZ,) + na, F32),
-            vm((2, 16, 512), F32), vm((8, 1024), F32),
-            vm((16, 512), F32), vm((8, 1024), F32), vm((2,) + nv, F32), vm((2,) + na, F32),
+            vm((NZ, 32, 512), F32), vm((NY - 1, NZ, 32, 512), BF), vm((NY - 1, NZ, 32, 512), BF),
+            vm((NZ, 32, 512), F32), vm((NZ - 1, 32, 512), BF), vm((NZ - 1, 32, 512), BF),
+            vm((2, 16, 512), F32), vm((16, 512), F32),
+            vm((NY, 32, 1024), F32), vm((NY, 32, 1024), BF), vm((NY, 32, 1024), BF),
+            vm((32, 1024), F32), vm((NY - 1, 32, 1024), BF), vm((NY - 1, 32, 1024), BF),
+            vm((NZ, 8, 512), F32), vm((NZ - 1, 8, 512), F32),
+            vm((NZ,) + nv, F32), vm((2,) + na, F32), vm((2,) + nv, F32), vm((NY,) + na, F32),
+            vm((NY,) + nv, F32), vm((NZ,) + na, F32),
             dma((5,)), dma((sends,)), dma((sends,)),
         ],
         cid=1, mib=58, smem=1, hbm=5,
@@ -637,7 +642,7 @@
             ((TOK, D), BF), ((1, D), F32), ((3, 4, DA), F32), ((4, DA), F32),
             ((HEADS, NREL), F32), ((1, 4 * D), F32), ((16, 512), F32),
         ],
-        mib=8,
+        mib=58,
     )
     return (
         lg.reshape(latent.shape),

time: 111 us -> 88.7 us (0.80)
  Pallas kernels: 105 us -> 87.8 us
  local copies, waits for them, and re-layouts: 3.99 us -> 0 us
    pallas_call x2, Pallas kernels: 105 us -> 87.8 us  [call(): pl.pallas_call(kernel, out_shape=[jax.ShapeDtypeStruct(s, d) for s, d in...]
    unnamed x12 -> x0, local copies, waits for them, and re-layouts: 3.99 us -> none
where the time goes in v4:
time: 88.7 us; the launch traced here: 88.4 us
  Pallas kernels  87.8 us (99%)
    pallas_call x2, Pallas kernels, call(): pl.pallas_call(kernel, out_shape=[jax.ShapeDtypeStruct(s, d) for s, d in...  87.8 us

profile of v4, /device:TPU:2, one launch (start us, length us, event | category | flops | bytes accessed | tf_op | source)
XLA Modules:
  0.0 88.4 jit_solution(6571415287983819189)
XLA Ops:
  0.6 85.2 %sublayer_backward.1 = (bf16[608,512]{1,0:T(8,128)(2,1)}, f32[16,512]{1,0:T(8,128)}, f32[8,512]{1,0:T(8,128)}, f32[8,768]{1,0:T(8,128)}, f32[1,512]{1,0:T(1,128)}) custom-call(s32[48]{0:T(128)} %pole_ref.1, s32[32,768]{1,0:T(8,128)} %constant.2.clone.maps, f32[4,759]{1,0:T(4,128)} %tab_ref.1, f32[1,512]{1,0:T(1,128)} %bitcast.14, f32[1,2048]{1,0:T(1,128)} %bitcast.13, ...), custom_call_target="tpu_custom_call" | custom-call | tf_op jit(solution)/shard_map/sublayer_backward/pallas_call | solution.py:141
  85.9 2.6 %finish.1 = (bf16[576,512]{1,0:T(8,128)(2,1)}, f32[1,512]{1,0:T(1,128)}, f32[3,4,256]{2,1,0:T(4,128)}, f32[4,256]{1,0:T(4,128)}, f32[4,759]{1,0:T(4,128)}, /*index=5*/f32[1,2048]{1,0:T(1,128)}, f32[16,512]{1,0:T(8,128)}) custom-call(s32[32,768]{1,0:T(8,128)} %constant.2.clone.maps, bf16[608,512]{1,0:T(8,128)(2,1)} %get-tuple-element.19.rp_ref, ...), custom_call_target="tpu_custom_call" | custom-call | tf_op jit(solution)/shard_map/finish/pallas_call | solution.py:141

commit v5 on v4

--- a/solution.py
+++ b/solution.py
@@ -190,7 +190,7 @@
     sm1, sq1, rm1, rq1, sv1, av1,
     am, sm2, rm2, bmm, sm3, rm3, cm, rm4,
     aq, sq2, rq2, bq, sq3, rq3, cq, rq4,
-    sv2, av2, sv3, av3, sv4, av4, ls, ss, rs,
+    sv2, sv3, sv4, av2, ls, ss, rs,
 ):
     lon, band, tp = lax.axis_index("lon"), lax.axis_index("lat"), lax.axis_index("tp")
     z, core = lax.div(lon, 2), lax.rem(lon, 2)
@@ -201,7 +201,13 @@
     y_devs = [(lon, lax.rem(yy + k, NY) * 2 + xx, tp) for k in range(1, NY)]
     z_devs = [(lax.rem(z + k, NZ) * 2 + core, band, tp) for k in range(1, NZ)]
     near = [device(s * o, s * a, 0) for s in (1, -1) for o, a in ((1, 0), (0, 1), (1, 1))]
-    partners = [peer, core_dev, x_dev] + y_devs + z_devs + near
+    group = [
+        (z * 2 + lax.rem(core + a, 2), lax.rem(yy + c, NY) * 2 + lax.rem(xx + b, 2), tp)
+        for a in range(2)
+        for b in range(2)
+        for c in range(NY)
+    ][1:]
+    partners = [peer] + group + z_devs + near
     barrier = pltpu.get_barrier_semaphore()
     for dev in partners:
         pl.semaphore_signal(barrier, inc=1, device_id=dev, device_id_type=MESH)
@@ -343,15 +349,18 @@
     build_bias(other)
     wait(pair)
     forward(other)
-    to_merge = pick(maps, PWM, TOK, TOK)
-    x = mm(pick(maps, PXM, TOK, 608), pc[...])
-    for g in range(2):
-        x = x + mm(mm(to_merge, ao[g]).astype(BF), pf[g])
-    y[...] = x.astype(BF)
-    yhc = [
-        links.send(y.at[480:576], yh.at[0], device(0, 1, 0)),
-        links.send(y.at[0:96], yh.at[1], device(0, -1, 0)),
-    ]
+    def residual(lo, hi):
+        to_merge = pick(maps, PWM, hi - lo, TOK, lo)
+        x = mm(pick(maps, PXM, hi - lo, 608, lo), pc[...])
+        for g in range(2):
+            x = x + mm(mm(to_merge, ao[g]).astype(BF), pf[g])
+        y[lo:hi, :] = x.astype(BF)
+
+    residual(0, 96)
+    yhc = [links.send(y.at[0:96], yh.at[1], device(0, -1, 0))]
+    residual(480, 576)
+    yhc.append(links.send(y.at[480:576], yh.at[0], device(0, 1, 0)))
+    residual(96, 480)
 
     wait(dmc)
     mgain = mgain_ref[...]
@@ -388,9 +397,12 @@
     for iz in range(NZ):
         part = mm_tn(mb[:, iz * 256 : (iz + 1) * 256], cmt[48:192, :])
         gm[iz] = part.reshape(2, NY, 32, 512)
-        for iy in range(NY):
+    turns = [lax.rem(yy + k, NY) for k in (1, 2, 3, 0)]
+    m1 = []
+    for iy in turns:
+        for iz in range(NZ):
             sm1[iy, iz] = gm[iz, 1 - core, iy].astype(BF)
-    m1 = [links.send(sm1, rm1, core_dev)]
+        m1.append(links.send(sm1.at[iy], rm1.at[iy], core_dev))
 
     dyw[...] = mm(pick(maps, PMW, TOK, TOK), dyt[...]).astype(BF)
     for g in range(2):
@@ -424,17 +436,16 @@
 
         lax.fori_loop(lo, hi, window, 0)
 
-    backward(tp, True, 0, 1)
-
-    wait(m1)
     m2 = []
     for k in range(1, NY):
-        iy = lax.rem(yy + k, NY)
+        wait(m1[k - 1 : k])
+        iy = turns[k - 1]
         for iz in range(NZ):
             sm2[k - 1, iz] = (gm[iz, core, iy] + rm1[iy, iz].astype(F32)).astype(BF)
         m2.append(links.send(sm2.at[k - 1], rm2.at[k - 1], y_devs[k - 1]))
-
-    backward(tp, True, 1)
+    wait(m1[3:])
+
+    backward(tp, True)
 
     dyp[...] = mm(dyw[...], features).astype(BF)
     for n in range(4):
@@ -507,8 +518,9 @@
             dh = dh + mm_nt(dqkv[g, n], wf[g, n])
     normed, inv = layer_stats(xw[...].astype(F32))
     av[...] = jnp.sum(dh * normed, 0, keepdims=True)
-    av1[core] = av[...]
-    a1 = [links.send(av1.at[core], av1.at[core], core_dev)]
+    me = (core * 2 + xx) * NY + yy
+    av1[me] = av[...]
+    a1 = [links.send(av1.at[me], av1.at[me], dev) for dev in group]
     branch = norm_back(dh, gain_ref[...], normed, inv).astype(BF)
     lg = (dyw[...].astype(F32) + branch.astype(F32)).astype(BF)
     lp[...] = mm(pick(maps, PPO, 608, TOK), lg).astype(BF)
@@ -524,10 +536,6 @@
         acc = acc + sv2[k]
     sv3[xx] = acc
     v3 = [links.send(sv3.at[xx], sv3.at[xx], x_dev)]
-    wait(a1)
-    av2[xx] = av1[0] + av1[1]
-    a2 = [links.send(av2.at[xx], av2.at[xx], x_dev)]
-
     wait(q3)
     acc = bq[...]
     for k in range(NY - 1):
@@ -539,9 +547,12 @@
     for k in range(1, NZ):
         q4.append(links.send(cq.at[lax.rem(z + k, NZ)], rq4.at[k - 1], z_devs[k - 1]))
 
-    wait(a2)
-    av3[yy] = av2[0] + av2[1]
-    a3 = [links.send(av3.at[yy], av3.at[yy], dev) for dev in y_devs]
+    wait(a1)
+    acc = av1[0]
+    for k in range(1, 4 * NY):
+        acc = acc + av1[k]
+    av2[z] = acc
+    a2 = [links.send(av2.at[z], av2.at[z], dev) for dev in z_devs]
     wait(v3)
     sv4[yy] = sv3[0] + sv3[1]
     v4 = [links.send(sv4.at[yy], sv4.at[yy], dev) for dev in y_devs]
@@ -553,9 +564,6 @@
     cm[0] = acc[0:16]
     cm[1] = acc[16:32]
     m4 = [links.send(cm.at[1 - xx], rm4, x_dev)]
-    wait(a3)
-    av4[z] = av3[0] + av3[1] + av3[2] + av3[3]
-    a4 = [links.send(av4.at[z], av4.at[z], dev) for dev in z_devs]
     wait(m4)
     om_ref[...] = cm[xx] + rm4[...]
     wait(q4)
@@ -565,10 +573,10 @@
     oq_ref[...] = acc
     wait(v4)
     ov_ref[...] = sv4[0] + sv4[1] + sv4[2] + sv4[3]
-    wait(a4)
-    acc = av4[0]
+    wait(a2)
+    acc = av2[0]
     for k in range(1, NZ):
-        acc = acc + av4[k]
+        acc = acc + av2[k]
     oa_ref[...] = acc
     wait(ro)
 
@@ -599,7 +607,7 @@
     vm = pltpu.VMEM
     nb = HEADS * WTOK
     nv, na = (8, 768), (1, D)
-    sends = 80
+    sends = 96
     rp, om, oq, ov, oa = call(
         kmain, "sublayer_backward",
         [
@@ -623,15 +631,14 @@
             vm((2, 2, NY, 32, 1024), F32), vm((608, D), BF), vm(nv, F32), vm(na, F32),
             vm((NY, NZ, 32, 512), BF), vm((2, NY, 32, 1024), BF),
             vm((NY, NZ, 32, 512), BF), vm((2, NY, 32, 1024), BF), vm((2,) + nv, F32),
-            vm((2,) + na, F32),
+            vm((4 * NY,) + na, F32),
             vm((NZ, 32, 512), F32), vm((NY - 1, NZ, 32, 512), BF), vm((NY - 1, NZ, 32, 512), BF),
             vm((NZ, 32, 512), F32), vm((NZ - 1, 32, 512), BF), vm((NZ - 1, 32, 512), BF),
             vm((2, 16, 512), F32), vm((16, 512), F32),
             vm((NY, 32, 1024), F32), vm((NY, 32, 1024), BF), vm((NY, 32, 1024), BF),
             vm((32, 1024), F32), vm((NY - 1, 32, 1024), BF), vm((NY - 1, 32, 1024), BF),
             vm((NZ, 8, 512), F32), vm((NZ - 1, 8, 512), F32),
-            vm((NZ,) + nv, F32), vm((2,) + na, F32), vm((2,) + nv, F32), vm((NY,) + na, F32),
-            vm((NY,) + nv, F32), vm((NZ,) + na, F32),
+            vm((NZ,) + nv, F32), vm((2,) + nv, F32), vm((NY,) + nv, F32), vm((NZ,) + na, F32),
             dma((5,)), dma((sends,)), dma((sends,)),
         ],
         cid=1, mib=58, smem=1, hbm=5,

time: 88.7 us -> 85.5 us (0.964)
  Pallas kernels: 87.8 us -> 83.8 us
    pallas_call x2, Pallas kernels: 87.8 us -> 83.8 us  [call(): pl.pallas_call(kernel, out_shape=[jax.ShapeDtypeStruct(s, d) for s, d in...]
where the time goes in v5:
time: 85.5 us; the launch traced here: 84.4 us
  Pallas kernels  83.8 us (98%)
    pallas_call x2, Pallas kernels, call(): pl.pallas_call(kernel, out_shape=[jax.ShapeDtypeStruct(s, d) for s, d in...  83.8 us

profile of v5, /device:TPU:2, one launch (start us, length us, event | category | flops | bytes accessed | tf_op | source)
XLA Modules:
  0.0 84.4 jit_solution(170349716752794408)
XLA Ops:
  0.6 81.2 %sublayer_backward.1 = (bf16[608,512]{1,0:T(8,128)(2,1)}, f32[16,512]{1,0:T(8,128)}, f32[8,512]{1,0:T(8,128)}, f32[8,768]{1,0:T(8,128)}, f32[1,512]{1,0:T(1,128)}) custom-call(s32[48]{0:T(128)} %pole_ref.1, s32[32,768]{1,0:T(8,128)} %constant.2.clone.maps, f32[4,759]{1,0:T(4,128)} %tab_ref.1, f32[1,512]{1,0:T(1,128)} %bitcast.14, f32[1,2048]{1,0:T(1,128)} %bitcast.13, ...), custom_call_target="tpu_custom_call" | custom-call | tf_op jit(solution)/shard_map/sublayer_backward/pallas_call | solution.py:141
  81.9 2.6 %finish.1 = (bf16[576,512]{1,0:T(8,128)(2,1)}, f32[1,512]{1,0:T(1,128)}, f32[3,4,256]{2,1,0:T(4,128)}, f32[4,256]{1,0:T(4,128)}, f32[4,759]{1,0:T(4,128)}, /*index=5*/f32[1,2048]{1,0:T(1,128)}, f32[16,512]{1,0:T(8,128)}) custom-call(s32[32,768]{1,0:T(8,128)} %constant.2.clone.maps, bf16[608,512]{1,0:T(8,128)(2,1)} %get-tuple-element.19.rp_ref, ...), custom_call_target="tpu_custom_call" | custom-call | tf_op jit(solution)/shard_map/finish/pallas_call | solution.py:141

commit v6 on v5

--- a/solution.py
+++ b/solution.py
@@ -24,6 +24,8 @@
 DA = HEADS * HD
 NREL = 759
 NZ, NY = 8, 4
+FAR_Y = (2, 1, 3)
+FAR_Z = (4, 3, 5, 2, 6, 1, 7)
 
 
 (QL, QL2, QC, QC2, PC, PXM, PXW, PWM, PMW, PPO, PF, FP, E0) = range(13)
@@ -397,7 +399,7 @@
     for iz in range(NZ):
         part = mm_tn(mb[:, iz * 256 : (iz + 1) * 256], cmt[48:192, :])
         gm[iz] = part.reshape(2, NY, 32, 512)
-    turns = [lax.rem(yy + k, NY) for k in (1, 2, 3, 0)]
+    turns = [lax.rem(yy + k, NY) for k in FAR_Y + (0,)]
     m1 = []
     for iy in turns:
         for iz in range(NZ):
@@ -437,9 +439,9 @@
         lax.fori_loop(lo, hi, window, 0)
 
     m2 = []
-    for k in range(1, NY):
-        wait(m1[k - 1 : k])
-        iy = turns[k - 1]
+    for n, k in enumerate(FAR_Y):
+        wait(m1[n : n + 1])
+        iy = turns[n]
         for iz in range(NZ):
             sm2[k - 1, iz] = (gm[iz, core, iy] + rm1[iy, iz].astype(F32)).astype(BF)
         m2.append(links.send(sm2.at[k - 1], rm2.at[k - 1], y_devs[k - 1]))
@@ -495,7 +497,7 @@
 
     wait(q2)
     q3 = []
-    for k in range(1, NY):
+    for k in FAR_Y:
         iy = lax.rem(yy + k, NY)
         sq3[k - 1] = (aq[iy] + rq2[iy].astype(F32)).astype(BF)
         q3.append(links.send(sq3.at[k - 1], rq3.at[k - 1], y_devs[k - 1]))
@@ -508,7 +510,7 @@
             acc = acc + rm2[k, iz].astype(F32)
         bmm[iz] = acc
     m3 = []
-    for k in range(1, NZ):
+    for k in FAR_Z:
         sm3[k - 1] = bmm[lax.rem(z + k, NZ)].astype(BF)
         m3.append(links.send(sm3.at[k - 1], rm3.at[k - 1], z_devs[k - 1]))
 
@@ -544,7 +546,7 @@
         rows = slice(iz * 4, iz * 4 + 4)
         cq[iz] = jnp.concatenate([acc[rows, 0:512], acc[rows, 512:1024]], 0)
     q4 = []
-    for k in range(1, NZ):
+    for k in FAR_Z:
         q4.append(links.send(cq.at[lax.rem(z + k, NZ)], rq4.at[k - 1], z_devs[k - 1]))
 
     wait(a1)

time: 85.5 us -> 85.2 us (level); the launches traced: 84.4 us -> 85 us
  no operation moved by 1% of the time
where the time goes in v6:
time: 85.2 us; the launch traced here: 85 us
  Pallas kernels  84.4 us (99%)
    pallas_call x2, Pallas kernels, call(): pl.pallas_call(kernel, out_shape=[jax.ShapeDtypeStruct(s, d) for s, d in...  84.4 us

profile of v6, /device:TPU:2, one launch (start us, length us, event | category | flops | bytes accessed | tf_op | source)
XLA Modules:
  0.0 85.0 jit_solution(18186739826818945369)
XLA Ops:
  0.6 81.8 %sublayer_backward.1 = (bf16[608,512]{1,0:T(8,128)(2,1)}, f32[16,512]{1,0:T(8,128)}, f32[8,512]{1,0:T(8,128)}, f32[8,768]{1,0:T(8,128)}, f32[1,512]{1,0:T(1,128)}) custom-call(s32[48]{0:T(128)} %pole_ref.1, s32[32,768]{1,0:T(8,128)} %constant.2.clone.maps, f32[4,759]{1,0:T(4,128)} %tab_ref.1, f32[1,512]{1,0:T(1,128)} %bitcast.14, f32[1,2048]{1,0:T(1,128)} %bitcast.13, ...), custom_call_target="tpu_custom_call" | custom-call | tf_op jit(solution)/shard_map/sublayer_backward/pallas_call | solution.py:143
  82.5 2.6 %finish.1 = (bf16[576,512]{1,0:T(8,128)(2,1)}, f32[1,512]{1,0:T(1,128)}, f32[3,4,256]{2,1,0:T(4,128)}, f32[4,256]{1,0:T(4,128)}, f32[4,759]{1,0:T(4,128)}, /*index=5*/f32[1,2048]{1,0:T(1,128)}, f32[16,512]{1,0:T(8,128)}) custom-call(s32[32,768]{1,0:T(8,128)} %constant.2.clone.maps, bf16[608,512]{1,0:T(8,128)(2,1)} %get-tuple-element.19.rp_ref, ...), custom_call_target="tpu_custom_call" | custom-call | tf_op jit(solution)/shard_map/finish/pallas_call | solution.py:143
